TPU v7x, 32 devices: a whole 2x2x4 slice. The times are simulated.
32 devices in a mesh: gx: 4 (over y, core), gy: 4 (over z), lev: 2 (over x).
Axes of the slice: x: 2, y: 2, z: 4, core: 2. Of those that a mesh axis runs over, the one named last changes fastest.
Arguments:
- model_state: float32 [2, 8, 2048, 2048], P(None, 'lev', 'gy', 'gx'), as said below
- cutoff: int32 [2, 8], P(None, 'lev'), may hold values from 5 to 10, as said below
- relax_rate: float32 [2, 8], P(None, 'lev'), may hold values from 0.2 to 1
- owner_map: int32 [2, 2], P('lev'), may hold values from 0 to 15
- era_store: float32 [16, 2, 8, 882], P(('gx', 'gy'), None, 'lev'), may hold values from -0.36 to 0.36
Outputs:
- nudged: float32 [2, 8, 2048, 2048], P(None, 'lev', 'gy', 'gx')
Inputs may be any that keep to these rules, and one draw needn't show every extreme that they name: `cutoff`: each draw holds both the smallest and the largest value somewhere. `model_state`: finite values of order one.
All inputs are finite; a program needn't handle non-finite values.
Results may differ from a plain program's by a relative error of at most 0.00007.
Values sent between devices are 32-bit elements; how exact they have to be, the bound alone decides.
No kernel may reach another device: no remote copies, remote signals or barrier semaphores. Data moves between devices by JAX's collectives and lax.ppermute only.
A program may use at most 64 MiB of HBM per device.

v0:
```python
import jax
import jax.numpy as jnp
from jax import lax
from jax.sharding import PartitionSpec as P

NX = 2048
NY = 2048
KC = 10
NK = 21


def from_root(value, axis, source):
    kept = jnp.where(lax.axis_index(axis) == source, value, 0).astype(value.dtype)
    return lax.psum(kept, axis)


def tables(positions, length):
    wave_index = jnp.arange(NK, dtype=jnp.int32) - KC
    turns = jnp.mod(positions[:, None] * wave_index[None, :], length).astype(jnp.float32)
    angle = turns * (6.2831855 / length)
    return (jnp.cos(angle), jnp.sin(angle))


def mix(form, left, right):
    return jnp.einsum(form, left, right, precision=lax.Precision.HIGHEST)


def forward_part(field, cos_y, sin_y, cos_x, sin_x):
    along_re = mix("vlyx,yk->vlkx", field, cos_y)
    along_im = -mix("vlyx,yk->vlkx", field, sin_y)
    part_re = mix("vlkx,xj->vlkj", along_re, cos_x) + mix("vlkx,xj->vlkj", along_im, sin_x)
    part_im = mix("vlkx,xj->vlkj", along_im, cos_x) - mix("vlkx,xj->vlkj", along_re, sin_x)
    return jnp.stack([part_re, part_im], axis=2) * (1.0 / (NX * NY))


def inverse_part(increment, cos_y, sin_y, cos_x, sin_x):
    delta_re = increment[:, :, 0]
    delta_im = increment[:, :, 1]
    back_re = mix("vlkj,xj->vlkx", delta_re, cos_x) - mix("vlkj,xj->vlkx", delta_im, sin_x)
    back_im = mix("vlkj,xj->vlkx", delta_re, sin_x) + mix("vlkj,xj->vlkx", delta_im, cos_x)
    return mix("vlkx,yk->vlyx", back_re, cos_y) - mix("vlkx,yk->vlyx", back_im, sin_y)


def body(model_state, cutoff, relax_rate, owner_map, era_store):
    nvar, levels, ny_local, nx_local = model_state.shape
    gx_pos = lax.axis_index("gx")
    gy_pos = lax.axis_index("gy")
    per_var = []
    for var_num in range(nvar):
        received = from_root(era_store, ("gx", "gy"), owner_map[0, var_num])
        per_var.append(received[0, var_num])
    analysis = jnp.stack(per_var).reshape(nvar, levels, 2, NK, NK)
    pencil = lax.all_to_all(model_state, "gy", split_axis=3, concat_axis=2, tiled=True)
    width = pencil.shape[3]
    y_pos = jnp.arange(NY, dtype=jnp.int32)
    x_pos = gx_pos * nx_local + gy_pos * width + jnp.arange(width, dtype=jnp.int32)
    cos_y, sin_y = tables(y_pos, NY)
    cos_x, sin_x = tables(x_pos, NX)
    partial_value = forward_part(pencil, cos_y, sin_y, cos_x, sin_x)
    spectrum = lax.psum(partial_value, ("gx", "gy"))
    wave_index = jnp.arange(NK, dtype=jnp.int32) - KC
    total_sq = wave_index[:, None] ** 2 + wave_index[None, :] ** 2
    keep = (total_sq[None, None] <= (cutoff**2)[:, :, None, None]).astype(jnp.float32)
    increment = relax_rate[:, :, None, None, None] * keep[:, :, None] * (analysis - spectrum)
    added = inverse_part(increment, cos_y, sin_y, cos_x, sin_x)
    return lax.all_to_all(pencil + added, "gy", split_axis=2, concat_axis=3, tiled=True)


def solution(mesh):
    placed = (
        P(None, "lev", "gy", "gx"),
        P(None, "lev"),
        P(None, "lev"),
        P("lev", None),
        P(("gx", "gy"), None, "lev", None),
    )
    return jax.shard_map(
        body, mesh=mesh, in_specs=placed, out_specs=P(None, "lev", "gy", "gx"), check_vma=False
    )
```

profile of v0, /device:TPU:0, one launch (start us, length us, event | category | flops | bytes accessed | tf_op | source)
XLA Modules:
  0.0 575.1 jit_solution(2396750115505021789)
XLA Ops:
  6.5 10.2 %copy.12 = f32[2,4,512,512]{2,1,0,3:T(4,128)} copy(f32[2,4,512,512]{3,2,1,0:T(8,128)} %param.5) | data formatting | bytes 16777216 | tf_op args[0]
  16.8 6.5 %all-to-all-start = ((f32[2,4,512,512]{2,1,0,3:T(4,128)}), f32[2,4,512,512]{2,1,0,3:T(4,128)}, u32[]{:S(2)}, u32[]{:S(2)}) async-start(f32[2,4,512,512]{2,1,0,3:T(4,128)} %copy.12), calls=%async_computation | async-start | bytes 16777216 | tf_op jit(solution)/shard_map/all_to_all | solution.py:53
  23.2 0.7 fusion.95
  25.2 0.1 broadcast_add_fusion
  25.3 0.6 broadcast_select_fusion.1
  25.9 181.4 %all-to-all-done = f32[2,4,512,512]{2,1,0,3:T(4,128)} async-done(((f32[2,4,512,512]{2,1,0,3:T(4,128)}), f32[2,4,512,512]{2,1,0,3:T(4,128)}, u32[]{:S(2)}, u32[]{:S(2)}) %all-to-all-start) | async-done | bytes 8388640 | tf_op jit(solution)/shard_map/all_to_all | solution.py:53
  207.3 10.0 %copy.13 = f32[2,4,512,4,128]{4,2,3,1,0:T(8,128)} copy(f32[2,4,512,4,128]{2,1,0,4,3:T(4,128)} %bitcast) | data formatting | bytes 16777216 | tf_op jit(solution)/shard_map/all_to_all | solution.py:53
  217.3 8.9 %fusion.2 = f32[2,4,21,128]{3,2,1,0:T(8,128)S(1)} fusion(f32[2,4,2048,128]{3,2,1,0:T(8,128)} %bitcast.71, s32[21]{0:T(128)S(1)} %iota_add_fusion.1), kind=kOutput, calls=%fused_computation.8 | convolution fusion | flops 529105920 | bytes 8474708 | tf_op jit(solution)/shard_map/vlyx,yk->vlkx/dot_general | solution.py:25
  226.3 4.8 convolution_bitcast_fusion
  231.1 0.4 fusion.34
  231.4 0.4 fusion.32
  231.8 0.4 fusion.1
  232.2 0.4 fusion
  232.5 0.7 maximum_multiply_fusion
  233.2 0.0 all-reduce.3.cloned.1.call-update
  233.2 0.1 compare_select_fusion
  233.3 88.1 %all-reduce.3.cloned.1.call-done = (f32[2,4,2,21,21]{4,3,1,0,2:T(8,128)}, f32[1,2,4,882]{3,2,1,0:T(4,128)}, f32[1,2,4,882]{3,2,1,0:T(4,128)}) async-done(((f32[2,4,2,21,21]{4,3,1,0,2:T(8,128)}, f32[1,2,4,882]{3,2,1,0:T(4,128)}, f32[1,2,4,882]{3,2,1,0:T(4,128)}), (f32[2,4,2,21,21]{4,3,1,0,2:T(8,128)}, f32[1,2,4,882]{3,2,1,0:T(4,128)}, f32[1,2,4,882]{3,2,1,0:T(4,128)})) %all-reduce.3.cloned.1.call-update) | async-done | bytes 84688 | tf_op jit(solution)/shard_map/psum | solution.py:60
  321.5 0.7 slice.25
  322.2 0.7 slice.24
  322.9 0.1 stack.16
  323.0 0.1 stack.17
  323.1 1.0 fusion.11
  324.1 0.3 fusion.21
  324.5 0.3 fusion.22
  324.8 0.3 convolution_add_fusion
  325.2 0.4 convolution_subtract_fusion
  325.5 7.9 %fusion.8 = f32[2048,2,4,128]{3,0,2,1:T(8,128)S(1)} fusion(f32[2,4,21,128]{3,2,1,0:T(8,128)S(1)} %convolution_subtract_fusion, s32[21]{0:T(128)S(1)} %iota_add_fusion.1), kind=kOutput, calls=%fused_computation.20 | convolution fusion | flops 529084416 | bytes 8474708 | tf_op jit(solution)/shard_map/vlkx,yk->vlyx/dot_general | solution.py:25
  333.4 10.8 %bitcast_add_fusion = f32[2,4,2048,128]{3,2,1,0:T(8,128)S(1)} fusion(f32[2,4,2048,128]{3,2,1,0:T(8,128)} %bitcast.72, f32[2048,2,4,128]{3,0,2,1:T(8,128)S(1)} %fusion.8, f32[2,4,21,128]{3,2,1,0:T(8,128)S(1)} %convolution_add_fusion, s32[21]{0:T(128)S(1)} %iota_add_fusion.1), kind=kOutput, calls=%fused_computation | convolution fusion | flops 533278720 | bytes 25251924 | tf_op jit(solution)/shard_map/vlkx,yk->vlyx/dot_general | solution.py:25
  344.2 13.7 %copy.16 = f32[2,4,2048,128]{3,1,0,2:T(4,128)S(1)} copy(f32[2,4,2048,128]{3,2,1,0:T(8,128)S(1)} %bitcast_add_fusion) | data formatting | bytes 16777216 | tf_op jit(solution)/shard_map/add | solution.py:66
  358.0 188.0 %all_to_all.36 = f32[2,4,2048,128]{3,1,0,2:T(4,128)} all-to-all(f32[2,4,2048,128]{3,1,0,2:T(4,128)S(1)} %copy.16), channel_id=1, replica_groups=mesh['gx'=4,'gy'=4,'lev'=2] {'gy'}, dimensions={2} | all-to-all | bytes 16777216 | tf_op jit(solution)/shard_map/all_to_all | solution.py:66
  545.9 12.0 %copy.17 = f32[2,4,512,4,128]{4,3,2,1,0:T(4,128)} copy(f32[2,4,512,4,128]{4,1,0,2,3:T(4,128)} %bitcast.74) | data formatting | bytes 16777216 | tf_op jit(solution)/shard_map/all_to_all | solution.py:66
  558.0 10.3 %all_to_all.33 = f32[2,4,512,512]{3,2,1,0:T(8,128)} reshape(f32[2,4,512,4,128]{4,3,2,1,0:T(4,128)} %copy.17) | data formatting | bytes 16777216 | tf_op jit(solution)/shard_map/all_to_all | solution.py:66
  (15 shorter events, 0.0 us)
Async XLA Ops:
  16.8 6.5 %copy-start.2 = (s32[2,4]{1,0:T(2,128)S(1)}, s32[2,4]{1,0:T(2,128)}, u32[]{:S(2)}) copy-start(s32[2,4]{1,0:T(2,128)} %param.6) | copy-start | bytes 100
  16.8 6.5 %copy-start.3 = (s32[1,2]{1,0:T(1,128)S(1)}, s32[1,2]{1,0:T(1,128)}, u32[]{:S(2)}) copy-start(s32[1,2]{1,0:T(1,128)} %param.8) | copy-start | bytes 28
  16.8 8.5 %copy-start.1 = (f32[1,2,4,882]{3,2,1,0:T(4,128)S(1)}, f32[1,2,4,882]{3,2,1,0:T(4,128)}, u32[]{:S(2)}) copy-start(f32[1,2,4,882]{3,2,1,0:T(4,128)} %param.9) | copy-start | bytes 84676
  16.8 190.5 %all-to-all-start = ((f32[2,4,512,512]{2,1,0,3:T(4,128)}), f32[2,4,512,512]{2,1,0,3:T(4,128)}, u32[]{:S(2)}, u32[]{:S(2)}) async-start(f32[2,4,512,512]{2,1,0,3:T(4,128)} %copy.12), calls=%async_computation | async-start | bytes 16777216 | tf_op jit(solution)/shard_map/all_to_all | solution.py:53
  23.2 298.2 %all-reduce.3.cloned.1.call-start = ((), (), s32[]{:S(2)}) async-start(), calls=%async_computation.2 | async-start | bytes 507904 | tf_op jit(solution)/shard_map/psum | solution.py:60
  217.3 8.9 %copy-start = (f32[2,4,512,4,128]{4,2,3,1,0:T(8,128)S(1)}, f32[2,4,512,4,128]{4,2,3,1,0:T(8,128)}, u32[]{:S(2)}) copy-start(f32[2,4,512,4,128]{4,2,3,1,0:T(8,128)} %copy.13) | copy-start | bytes 25165828
  217.3 15.9 %copy-start.4 = (f32[2,4]{1,0:T(2,128)S(1)}, f32[2,4]{1,0:T(2,128)}, u32[]{:S(2)}) copy-start(f32[2,4]{1,0:T(2,128)} %param.7) | copy-start | bytes 100
Sparse Core Ops, SparseCore 0:
  233.4 88.0 all-reduce.2
where the time goes:
time: 576 us; the launch traced here: 575 us
  waiting for transfers between devices  270 us (47%)
  blocking collectives  188 us (33%)
  local copies, waits for them, and re-layouts  58.5 us (10%)
  matrix products  35.3 us (6%)
  between operations  14.8 us (3%)
  starting transfers between devices  6.46 us (1%)
    all_to_all x1, blocking collectives, body(): lax.all_to_all(pencil + added, 'gy', split_axis=2, concat_axis=3, tiled=T...  188 us
    all_to_all x1, waiting for transfers between devices, body(): lax.all_to_all(model_state, 'gy', split_axis=3, concat_axis=2, tiled=True)  181 us
    psum x1, waiting for transfers between devices, body(): spectrum = lax.psum(partial_value, ('gx', 'gy'))  88.1 us
    dot_general x12, matrix products, mix(): return jnp.einsum(form, left, right, precision=lax.Precision.HIGHEST)  35.3 us
    all_to_all x2, local copies, waits for them, and re-layouts, body(): lax.all_to_all(pencil + added, 'gy', split_axis=2, concat_axis=3, tiled=T...  22.3 us
    add x1, local copies, waits for them, and re-layouts, body(): pencil + added  13.7 us
  transfers between devices with their start and end apart: 2, of which 2 were waited for; matrix products, arithmetic and copies ran while one was open for 0% of the time, Pallas kernels for 0%

commit v1 on v0

v1 whole, which is shorter than its diff:
```python
import functools

import jax
import jax.numpy as jnp
import ml_dtypes
import numpy as np
from jax import lax
from jax.experimental import pallas as pl
from jax.experimental.pallas import tpu as pltpu
from jax.sharding import PartitionSpec as P

NX = 2048
NY = 2048
KC = 10
NK = 21
F = 8
GROUP = 32
SLOTS = 24
PACKED = SLOTS * GROUP


def basis(positions, length):
    wave = np.concatenate([np.arange(KC + 1), np.arange(1, KC + 1)])
    angle = np.mod(positions[:, None] * wave[None, :], length) * (2 * np.pi / length)
    return np.where(np.arange(NK) <= KC, np.cos(angle), np.sin(angle))


def halves(table):
    high = table.astype(ml_dtypes.bfloat16)
    low = (table - high.astype(np.float64)).astype(ml_dtypes.bfloat16)
    return high, low


def forward_tables(n_gx, n_gy):
    weight = np.where(np.arange(NK) == 0, 1.0, 2.0)
    high, low = halves(basis(np.arange(NY), NY) * weight / NY)
    ny = NY // n_gy
    along_y = np.zeros((n_gy, 64, ny), ml_dtypes.bfloat16)
    along_y[:, :NK] = high.reshape(n_gy, ny, NK).transpose(0, 2, 1)
    along_y[:, 32 : 32 + NK] = low.reshape(n_gy, ny, NK).transpose(0, 2, 1)
    high, low = halves(basis(np.arange(NX), NX) * weight / NX)
    nx = NX // n_gx
    along_x = np.zeros((n_gx, nx, 256), ml_dtypes.bfloat16)
    for group in range(4):
        at = group * GROUP
        along_x[:, :, at : at + NK] = high.reshape(n_gx, nx, NK)
        along_x[:, :, 128 + at : 128 + at + NK] = low.reshape(n_gx, nx, NK)
    return along_y, along_x


def inverse_tables(n_gx, n_gy):
    high, low = halves(basis(np.arange(NY), NY))
    ny = NY // n_gy
    along_y = np.zeros((n_gy, ny, 128), ml_dtypes.bfloat16)
    for slot in range(NK):
        at = (slot % 4) * (SLOTS // 4) + slot // 4
        along_y[:, :, at] = high[:, slot].reshape(n_gy, ny)
        along_y[:, :, SLOTS + at] = low[:, slot].reshape(n_gy, ny)
        along_y[:, :, 2 * SLOTS + at] = high[:, slot].reshape(n_gy, ny)
    high, low = halves(basis(np.arange(NX), NX))
    nx = NX // n_gx
    along_x = np.zeros((n_gx, 256, nx), ml_dtypes.bfloat16)
    for group in range(4):
        at = group * GROUP
        along_x[:, at : at + NK] = high.reshape(n_gx, nx, NK).transpose(0, 2, 1)
        along_x[:, 128 + at : 128 + at + NK] = low.reshape(n_gx, nx, NK).transpose(0, 2, 1)
    return along_y, along_x


def split(value):
    high = value.astype(jnp.bfloat16)
    return high, (value - high.astype(jnp.float32)).astype(jnp.bfloat16)


def dot(left, right):
    return jnp.dot(left, right, preferred_element_type=jnp.float32)


def lane_group(shape):
    return lax.broadcasted_iota(jnp.int32, shape, 1) // GROUP


def analysis_rows(store):
    pieces = []
    for row in range(2 * NK):
        at = row * NK
        base = at // 128 * 128
        off = at - base
        width = 128 if off + NK <= 128 else 256
        window = store[:, base : base + width]
        pieces.append(pltpu.roll(window, (width - off) % width, 1)[:, :128] if off else window[:, :128])
    high, low = split(jnp.concatenate(pieces, axis=0))
    wave = lax.broadcasted_iota(jnp.int32, (128, 128), 0) - KC
    column = lax.broadcasted_iota(jnp.int32, (128, 128), 1) % GROUP
    number = jnp.where(column <= KC, column, column - KC)
    plus = jnp.where(wave == number, 1.0, 0.0)
    minus = jnp.where((wave == -number) & (number > 0), 1.0, 0.0)
    fold = jnp.where(column <= KC, plus + minus, plus - minus)
    fold = jnp.where(column < NK, fold, 0.0).astype(jnp.bfloat16)
    folded = dot(high, fold) + dot(low, fold)
    part = [folded[8 * row : 8 * row + 8] for row in range(2 * NK)]
    real, imag = part[:NK], part[NK:]
    even = lax.broadcasted_iota(jnp.int32, (8, 128), 1) % GROUP <= KC
    rows = [jnp.where(even, real[KC], -imag[KC])]
    for wave in range(1, KC + 1):
        up, down = KC + wave, KC - wave
        rows.append(jnp.where(even, real[up] + real[down], -(imag[up] + imag[down])))
    for wave in range(1, KC + 1):
        up, down = KC + wave, KC - wave
        rows.append(-jnp.where(even, imag[up] - imag[down], real[up] - real[down]))
    return rows


def pack(rows):
    group = lane_group((8, 128))
    blocks = []
    for block in range(SLOTS // 4):
        total = jnp.zeros((8, 128), jnp.float32)
        for j in range(4):
            if 4 * block + j < len(rows):
                total = jnp.where(group == j, rows[4 * block + j], total)
        blocks.append(total)
    return jnp.concatenate(blocks, axis=1)


def per_field(values):
    row = lax.broadcasted_iota(jnp.int32, (F, 1), 0)
    total = jnp.full((F, 1), values[0])
    for field in range(1, F):
        total = jnp.where(row == field, values[field], total)
    return total


def project_kernel(
    n_gy, levels, owner, cutoff, relax, era, field_hbm, fy_hbm, fx_hbm, iy_hbm, ix_hbm,
    share, field, iy, ix, store, fy, fx, bands, field_sem, table_sem,
):
    gx, gy = lax.axis_index("gx"), lax.axis_index("gy")
    tables = [
        pltpu.make_async_copy(src, dst, table_sem.at[n])
        for n, (src, dst) in enumerate(
            ((fy_hbm.at[gy], fy), (fx_hbm.at[gx], fx), (iy_hbm.at[gy], iy), (ix_hbm.at[gx], ix))
        )
    ]
    tables[0].start()
    for f in range(F):
        pltpu.make_async_copy(field_hbm.at[f // levels, f % levels], field.at[f], field_sem.at[f]).start()
    for copy in tables[1:]:
        copy.start()

    store[...] = jnp.zeros_like(store)
    for var in range(F // levels):
        store[var * levels : (var + 1) * levels, : 2 * NK * NK] = era[0, var]
    analysis = pack(analysis_rows(store[...]))
    me = gx * n_gy + gy
    mine = per_field([(owner[0, f // levels] == me).astype(jnp.int32) for f in range(F)])
    limit = per_field([cutoff[f // levels, f % levels] for f in range(F)])
    rate = per_field([relax[f // levels, f % levels] for f in range(F)])
    lane = lax.broadcasted_iota(jnp.int32, (F, PACKED), 1)
    slot, column = lane // GROUP, lane % GROUP
    ky = jnp.where(slot <= KC, slot, slot - KC)
    kx = jnp.where(column <= KC, column, column - KC)
    factor = jnp.where(ky * ky + kx * kx <= limit * limit, rate, 0.0)
    analysis = jnp.where(mine == 1, analysis, 0.0)

    tables[0].wait()

    def one(f, _):
        pltpu.make_async_copy(field_hbm.at[0, 0], field.at[f], field_sem.at[f]).wait()
        high, low = split(field[f])
        wide = dot(fy[...], high)
        band = wide[:SLOTS] + wide[32 : 32 + SLOTS] + dot(fy[:32], low)[:SLOTS]
        for tile in range(bands.shape[0]):
            bands[tile, pl.ds(f, SLOTS, stride=F), :] = band[:, 128 * tile : 128 * tile + 128]
        return 0

    lax.fori_loop(0, F, one, 0)
    tables[1].wait()
    high, low = split(jnp.concatenate([bands[tile] for tile in range(bands.shape[0])], axis=1))
    both = dot(high, fx[...])
    spectrum = both[:, :128] + both[:, 128:] + dot(low, fx[:, :128])
    spectrum = pack([spectrum[F * slot : F * slot + F] for slot in range(SLOTS)])
    share[...] = factor * (analysis - spectrum)
    tables[2].wait()
    tables[3].wait()


def nudge_kernel(levels, chunk, mine, other, field, iy, ix, out_hbm, out, bands, sem):
    total = mine[...] + other[...]
    group = lane_group((F, 128))
    rows = []
    for j in range(4):
        for block in range(SLOTS // 4):
            rows.append(jnp.where(group == j, total[:, 128 * block : 128 * block + 128], 0.0))
    high, low = split(jnp.concatenate(rows, axis=0))
    wide = dot(high, ix[:128]) + dot(high, ix[128:]) + dot(low, ix[:128])
    for tile in range(bands.shape[0]):
        bands[tile] = wide[:, 128 * tile : 128 * tile + 128]
    ny, nx = out.shape[1:]
    steps = ny // chunk

    def one(f, _):
        band = [bands[tile, pl.ds(f, SLOTS, stride=F), :] for tile in range(bands.shape[0])]
        band = jnp.concatenate(band, axis=1)
        high = band.astype(jnp.bfloat16).astype(jnp.float32)
        stacked = jnp.concatenate([high, high, band - high, jnp.zeros((128 - 3 * SLOTS, nx), jnp.float32)], axis=0)
        stacked = stacked.astype(jnp.bfloat16)
        for step in range(steps):
            at = pl.ds(step * chunk, chunk)
            out[f, at] = field[f, at] + dot(iy[at], stacked)
            pltpu.make_async_copy(
                out.at[f, at], out_hbm.at[f // levels, f % levels, at], sem.at[f * steps + step]
            ).start()
        return 0

    lax.fori_loop(0, F, one, 0)

    def end(n, _):
        f, step = n // steps, n % steps
        at = pl.ds(pl.multiple_of(step * chunk, chunk), chunk)
        pltpu.make_async_copy(out.at[f, at], out_hbm.at[f // levels, f % levels, at], sem.at[n]).wait()
        return 0

    lax.fori_loop(0, F * steps, end, 0)


def swap(value, axis, size, bit):
    return lax.ppermute(value, axis, [(i, i ^ bit) for i in range(size)])


def body(n_gx, n_gy, model_state, cutoff, relax_rate, owner_map, era_store):
    nvar, levels, ny, nx = model_state.shape
    fy, fx = forward_tables(n_gx, n_gy)
    iy, ix = inverse_tables(n_gx, n_gy)
    smem = pl.BlockSpec(memory_space=pltpu.SMEM)
    vmem = pl.BlockSpec(memory_space=pltpu.VMEM)
    hbm = pl.BlockSpec(memory_space=pl.ANY)
    share, field, iy, ix = pl.pallas_call(
        functools.partial(project_kernel, n_gy, levels),
        out_shape=(
            pltpu.VMEM((F, PACKED), jnp.float32),
            pltpu.VMEM((F, ny, nx), jnp.float32),
            pltpu.VMEM((ny, 128), jnp.bfloat16),
            pltpu.VMEM((256, nx), jnp.bfloat16),
        ),
        in_specs=[smem, smem, smem, vmem, hbm, hbm, hbm, hbm, hbm],
        out_specs=[vmem] * 4,
        scratch_shapes=[
            pltpu.VMEM((F, 1024), jnp.float32),
            pltpu.VMEM((64, ny), jnp.bfloat16),
            pltpu.VMEM((nx, 256), jnp.bfloat16),
            pltpu.VMEM((nx // 128, SLOTS * F, 128), jnp.float32),
            pltpu.SemaphoreType.DMA((F,)),
            pltpu.SemaphoreType.DMA((4,)),
        ],
        compiler_params=pltpu.CompilerParams(vmem_limit_bytes=20 * 2**20),
        name="project",
    )(owner_map, cutoff, relax_rate, era_store, model_state, fy, fx, iy, ix)

    steps = [("gx", n_gx, 1 << bit) for bit in range(n_gx.bit_length() - 1)]
    steps += [("gy", n_gy, 1 << bit) for bit in range(n_gy.bit_length() - 1)]
    for step in steps[:-1]:
        share = share + swap(share, *step)
    other = swap(share, *steps[-1])

    chunk = min(ny, 256)
    nudged = pl.pallas_call(
        functools.partial(nudge_kernel, levels, chunk),
        out_shape=jax.ShapeDtypeStruct(model_state.shape, jnp.float32),
        in_specs=[vmem] * 5,
        out_specs=hbm,
        scratch_shapes=[
            pltpu.VMEM((F, ny, nx), jnp.float32),
            pltpu.VMEM((nx // 128, SLOTS * F, 128), jnp.float32),
            pltpu.SemaphoreType.DMA((F * (ny // chunk),)),
        ],
        compiler_params=pltpu.CompilerParams(vmem_limit_bytes=30 * 2**20),
        name="nudge",
    )(share, other, field, iy, ix)
    return nudged


def solution(mesh):
    n_gx, n_gy = mesh.shape["gx"], mesh.shape["gy"]
    placed = (
        P(None, "lev", "gy", "gx"),
        P(None, "lev"),
        P(None, "lev"),
        P("lev", None),
        P(("gx", "gy"), None, "lev", None),
    )
    return jax.shard_map(
        functools.partial(body, n_gx, n_gy),
        mesh=mesh,
        in_specs=placed,
        out_specs=P(None, "lev", "gy", "gx"),
        check_vma=False,
    )
```

time: 576 us -> 34.3 us (0.06)
  waiting for transfers between devices: 270 us -> 6.26 us
  blocking collectives: 188 us -> 0 us
  local copies, waits for them, and re-layouts: 58.5 us -> 10.6 us
  matrix products: 35.3 us -> 0 us
  between operations: 14.8 us -> 0.02 us
  Pallas kernels: 0 us -> 8.5 us
    all_to_all x1 -> x0, blocking collectives: 188 us -> none  [body(): lax.all_to_all(pencil + added, 'gy', split_axis=2, concat_axis=3, tiled=T...]
    all_to_all x1 -> x0, waiting for transfers between devices: 181 us -> none  [body(): lax.all_to_all(model_state, 'gy', split_axis=3, concat_axis=2, tiled=True)]
    psum x1 -> x0, waiting for transfers between devices: 88.1 us -> none  [body(): spectrum = lax.psum(partial_value, ('gx', 'gy'))]
    dot_general x12 -> x0, matrix products: 35.3 us -> none  [mix(): return jnp.einsum(form, left, right, precision=lax.Precision.HIGHEST)]
    all_to_all x3 -> x0, local copies, waits for them, and re-layouts: 32.3 us -> none  [the longest x2 22.3 us: body(): lax.all_to_all(pencil + added, 'gy', split_axis=2, concat_axis=3, tiled=T...]
    add x1 -> x0, local copies, waits for them, and re-layouts: 13.7 us -> none  [body(): pencil + added]
    pallas_call x0 -> x2, Pallas kernels: none -> 8.5 us  [the longest x1 4.57 us: body(): pl.pallas_call(functools.partial(project_kernel, n_gy, levels), out_shape...]
    ppermute x0 -> x4, starting transfers between devices: none -> 8.49 us  [swap(): return lax.ppermute(value, axis, [(i, i ^ bit) for i in range(size)])]
  transfers between devices with their start and end apart: 2 -> 4, of which waited for: 2 -> 4; matrix products, arithmetic and copies ran while one was open for 0% -> 0% of each run, Pallas kernels for 0% -> 0%
where the time goes in v1:
time: 34.3 us; the launch traced here: 33.9 us
  local copies, waits for them, and re-layouts  10.6 us (31%)
  Pallas kernels  8.5 us (25%)
  starting transfers between devices  8.49 us (25%)
  waiting for transfers between devices  6.26 us (18%)
    unnamed x18, local copies, waits for them, and re-layouts  10.6 us
    ppermute x4, starting transfers between devices, swap(): return lax.ppermute(value, axis, [(i, i ^ bit) for i in range(size)])  8.49 us
    ppermute x4, waiting for transfers between devices, swap(): return lax.ppermute(value, axis, [(i, i ^ bit) for i in range(size)])  6.26 us
    pallas_call x1, Pallas kernels, body(): pl.pallas_call(functools.partial(project_kernel, n_gy, levels), out_shape...  4.57 us
    pallas_call x1, Pallas kernels, body(): pl.pallas_call(functools.partial(nudge_kernel, levels, chunk), out_shape=...  3.93 us
  transfers between devices with their start and end apart: 4, of which 4 were waited for; matrix products, arithmetic and copies ran while one was open for 0% of the time, Pallas kernels for 0%

profile of v1, /device:TPU:0, one launch (start us, length us, event | category | flops | bytes accessed | tf_op | source)
XLA Modules:
  0.0 33.9 jit_solution(6231435124449299664)
XLA Ops:
  0.0 0.0 copy-start
  0.0 3.4 %copy-done = f32[2,4,512,512]{3,2,1,0:T(8,128)S(1)} copy-done((f32[2,4,512,512]{3,2,1,0:T(8,128)S(1)}, f32[2,4,512,512]{3,2,1,0:T(8,128)}, u32[]{:S(2)}) %copy-start) | copy-done | bytes 8388632
  3.4 0.0 copy-start.1
  3.4 1.2 %copy-done.1 = bf16[4,256,512]{2,1,0:T(8,128)(2,1)S(1)} copy-done((bf16[4,256,512]{2,1,0:T(8,128)(2,1)S(1)}, bf16[4,256,512]{2,1,0:T(8,128)(2,1)}, u32[]{:S(2)}) %copy-start.1) | copy-done | bytes 1048600
  4.6 0.0 copy-start.2
  4.6 1.2 %copy-done.2 = bf16[4,512,256]{2,1,0:T(8,128)(2,1)S(1)} copy-done((bf16[4,512,256]{2,1,0:T(8,128)(2,1)S(1)}, bf16[4,512,256]{2,1,0:T(8,128)(2,1)}, u32[]{:S(2)}) %copy-start.2) | copy-done | bytes 1048600
  5.8 0.0 copy-start.3
  5.8 1.0 %copy-done.3 = bf16[4,512,128]{2,1,0:T(8,128)(2,1)S(1)} copy-done((bf16[4,512,128]{2,1,0:T(8,128)(2,1)S(1)}, bf16[4,512,128]{2,1,0:T(8,128)(2,1)}, u32[]{:S(2)}) %copy-start.3) | copy-done | bytes 524312
  6.9 0.0 copy-start.4
  6.9 0.9 %copy-done.4 = bf16[4,64,512]{2,1,0:T(8,128)(2,1)S(1)} copy-done((bf16[4,64,512]{2,1,0:T(8,128)(2,1)S(1)}, bf16[4,64,512]{2,1,0:T(8,128)(2,1)}, u32[]{:S(2)}) %copy-start.4) | copy-done | bytes 262168
  7.8 0.0 copy-start.5
  7.8 0.7 %copy-done.5 = f32[1,2,4,882]{3,2,1,0:T(4,128)S(1)} copy-done((f32[1,2,4,882]{3,2,1,0:T(4,128)S(1)}, f32[1,2,4,882]{3,2,1,0:T(4,128)}, u32[]{:S(2)}) %copy-start.5) | copy-done | bytes 28248
  8.6 0.0 copy-start.6
  8.6 0.7 %copy-done.6 = s32[2,4]{1,0:T(2,128)S(1)} copy-done((s32[2,4]{1,0:T(2,128)S(1)}, s32[2,4]{1,0:T(2,128)}, u32[]{:S(2)}) %copy-start.6) | copy-done | bytes 56
  9.3 0.0 copy-start.7
  9.3 0.7 %copy-done.7 = f32[2,4]{1,0:T(2,128)S(1)} copy-done((f32[2,4]{1,0:T(2,128)S(1)}, f32[2,4]{1,0:T(2,128)}, u32[]{:S(2)}) %copy-start.7) | copy-done | bytes 56
  9.9 0.0 copy-start.8
  9.9 0.7 %copy-done.8 = s32[1,2]{1,0:T(1,128)S(1)} copy-done((s32[1,2]{1,0:T(1,128)S(1)}, s32[1,2]{1,0:T(1,128)}, u32[]{:S(2)}) %copy-start.8) | copy-done | bytes 32
  10.6 4.6 %project.1 = (f32[8,768]{1,0:T(8,128)S(1)}, f32[8,512,512]{2,1,0:T(8,128)S(1)}, bf16[512,128]{1,0:T(8,128)(2,1)S(1)}, bf16[256,512]{1,0:T(8,128)(2,1)S(1)}) custom-call(s32[1,2]{1,0:T(1,128)S(1)} %copy-done.8, s32[2,4]{1,0:T(2,128)S(1)} %copy-done.6, f32[2,4]{1,0:T(2,128)S(1)} %copy-done.7, f32[1,2,4,882]{3,2,1,0:T(4,128)S(1)} %copy-done.5, ...), custom_call_target="tpu_custom_call" | custom-call | tf_op jit(solution)/shard_map/project/pallas_call | solution.py:238
  15.2 0.5 %collective-permute-start = (f32[8,768]{1,0:T(8,128)S(1)}, f32[8,768]{1,0:T(8,128)S(1)}, u32[]{:S(2)}, u32[]{:S(2)}) collective-permute-start(f32[8,768]{1,0:T(8,128)S(1)} %get-tuple-element.9), channel_id=1, source_target_pairs={{0,8},{8,0},{16,24},{24,16},{1,9},{9,1},{17,25},{25,17},{2,10},{10... | collective-permute-start | bytes 73736 | tf_op jit(solution)/shard_map/ppermute | solution.py:228
  15.7 0.8 %collective-permute-done = f32[8,768]{1,0:T(8,128)S(1)} collective-permute-done((f32[8,768]{1,0:T(8,128)S(1)}, f32[8,768]{1,0:T(8,128)S(1)}, u32[]{:S(2)}, u32[]{:S(2)}) %collective-permute-start) | collective-permute-done | bytes 24608 | tf_op jit(solution)/shard_map/ppermute | solution.py:228
  16.5 2.9 %collective-permute-start.1 = (f32[8,768]{1,0:T(8,128)S(1)}, f32[8,768]{1,0:T(8,128)S(1)}, u32[]{:S(2)}, u32[]{:S(2)}) collective-permute-start(f32[8,768]{1,0:T(8,128)S(1)} %add.9), channel_id=1, source_target_pairs={{0,16},{8,24},{16,0},{24,8},{1,17},{9,25},{17,1},{25,9},{2,18},{10... | collective-permute-start | bytes 73736 | tf_op jit(solution)/shard_map/ppermute | solution.py:228
  19.4 1.8 %collective-permute-done.1 = f32[8,768]{1,0:T(8,128)S(1)} collective-permute-done((f32[8,768]{1,0:T(8,128)S(1)}, f32[8,768]{1,0:T(8,128)S(1)}, u32[]{:S(2)}, u32[]{:S(2)}) %collective-permute-start.1) | collective-permute-done | bytes 24608 | tf_op jit(solution)/shard_map/ppermute | solution.py:228
  21.2 2.1 %collective-permute-start.2 = (f32[8,768]{1,0:T(8,128)S(1)}, f32[8,768]{1,0:T(8,128)S(1)}, u32[]{:S(2)}, u32[]{:S(2)}) collective-permute-start(f32[8,768]{1,0:T(8,128)S(1)} %add.10), channel_id=1, source_target_pairs={{0,2},{2,0},{4,6},{6,4},{1,3},{3,1},{5,7},{7,5},{8,10},{10,8},{12,... | collective-permute-start | bytes 73736 | tf_op jit(solution)/shard_map/ppermute | solution.py:228
  23.3 1.8 %collective-permute-done.2 = f32[8,768]{1,0:T(8,128)S(1)} collective-permute-done((f32[8,768]{1,0:T(8,128)S(1)}, f32[8,768]{1,0:T(8,128)S(1)}, u32[]{:S(2)}, u32[]{:S(2)}) %collective-permute-start.2) | collective-permute-done | bytes 24608 | tf_op jit(solution)/shard_map/ppermute | solution.py:228
  25.1 3.0 %collective-permute-start.3 = (f32[8,768]{1,0:T(8,128)S(1)}, f32[8,768]{1,0:T(8,128)S(1)}, u32[]{:S(2)}, u32[]{:S(2)}) collective-permute-start(f32[8,768]{1,0:T(8,128)S(1)} %add.11.mine), channel_id=1, source_target_pairs={{0,4},{2,6},{4,0},{6,2},{1,5},{3,7},{5,1},{7,3},{8,12},{10,14},{12... | collective-permute-start | bytes 73736 | tf_op jit(solution)/shard_map/ppermute | solution.py:228
  28.1 1.8 %collective-permute-done.3.other = f32[8,768]{1,0:T(8,128)S(1)} collective-permute-done((f32[8,768]{1,0:T(8,128)S(1)}, f32[8,768]{1,0:T(8,128)S(1)}, u32[]{:S(2)}, u32[]{:S(2)}) %collective-permute-start.3) | collective-permute-done | bytes 24608 | tf_op jit(solution)/shard_map/ppermute | solution.py:228
  29.9 3.9 %nudge.1 = f32[2,4,512,512]{3,2,1,0:T(8,128)} custom-call(f32[8,768]{1,0:T(8,128)S(1)} %add.11.mine, f32[8,768]{1,0:T(8,128)S(1)} %collective-permute-done.3.other, f32[8,512,512]{2,1,0:T(8,128)S(1)} %get-tuple-element.10.field, bf16[512,128]{1,0:T(8,128)(2,1)S(1)} %get-tuple-element.11.iy, bf16[256,512]{1,0:T(8,128)(2,1)S(1)} %get-tuple-element.12.ix), custom_call_target="tpu_custom_call" | custom-call | tf_op jit(solution)/shard_map/nudge/pallas_call | solution.py:267
  (3 shorter events, 0.0 us)
Async XLA Ops:
  0.0 3.4 %copy-start = (f32[2,4,512,512]{3,2,1,0:T(8,128)S(1)}, f32[2,4,512,512]{3,2,1,0:T(8,128)}, u32[]{:S(2)}) copy-start(f32[2,4,512,512]{3,2,1,0:T(8,128)} %field_hbm.1) | copy-start | bytes 25165828
  3.4 1.2 %copy-start.1 = (bf16[4,256,512]{2,1,0:T(8,128)(2,1)S(1)}, bf16[4,256,512]{2,1,0:T(8,128)(2,1)}, u32[]{:S(2)}) copy-start(bf16[4,256,512]{2,1,0:T(8,128)(2,1)} %constant.11.clone.ix_hbm) | copy-start | bytes 3145732
  4.6 1.2 %copy-start.2 = (bf16[4,512,256]{2,1,0:T(8,128)(2,1)S(1)}, bf16[4,512,256]{2,1,0:T(8,128)(2,1)}, u32[]{:S(2)}) copy-start(bf16[4,512,256]{2,1,0:T(8,128)(2,1)} %constant.9.clone.fx_hbm) | copy-start | bytes 3145732
  5.8 1.0 %copy-start.3 = (bf16[4,512,128]{2,1,0:T(8,128)(2,1)S(1)}, bf16[4,512,128]{2,1,0:T(8,128)(2,1)}, u32[]{:S(2)}) copy-start(bf16[4,512,128]{2,1,0:T(8,128)(2,1)} %constant.10.clone.iy_hbm) | copy-start | bytes 1572868
  6.9 0.9 %copy-start.4 = (bf16[4,64,512]{2,1,0:T(8,128)(2,1)S(1)}, bf16[4,64,512]{2,1,0:T(8,128)(2,1)}, u32[]{:S(2)}) copy-start(bf16[4,64,512]{2,1,0:T(8,128)(2,1)} %constant.8.clone.fy_hbm) | copy-start | bytes 786436
  7.8 0.7 %copy-start.5 = (f32[1,2,4,882]{3,2,1,0:T(4,128)S(1)}, f32[1,2,4,882]{3,2,1,0:T(4,128)}, u32[]{:S(2)}) copy-start(f32[1,2,4,882]{3,2,1,0:T(4,128)} %era.1) | copy-start | bytes 84676
  8.6 0.7 %copy-start.6 = (s32[2,4]{1,0:T(2,128)S(1)}, s32[2,4]{1,0:T(2,128)}, u32[]{:S(2)}) copy-start(s32[2,4]{1,0:T(2,128)} %cutoff.1) | copy-start | bytes 100
  9.3 0.7 %copy-start.7 = (f32[2,4]{1,0:T(2,128)S(1)}, f32[2,4]{1,0:T(2,128)}, u32[]{:S(2)}) copy-start(f32[2,4]{1,0:T(2,128)} %relax.1) | copy-start | bytes 100
  9.9 0.7 %copy-start.8 = (s32[1,2]{1,0:T(1,128)S(1)}, s32[1,2]{1,0:T(1,128)}, u32[]{:S(2)}) copy-start(s32[1,2]{1,0:T(1,128)} %owner.1) | copy-start | bytes 28
  15.2 1.4 %collective-permute-start = (f32[8,768]{1,0:T(8,128)S(1)}, f32[8,768]{1,0:T(8,128)S(1)}, u32[]{:S(2)}, u32[]{:S(2)}) collective-permute-start(f32[8,768]{1,0:T(8,128)S(1)} %get-tuple-element.9), channel_id=1, source_target_pairs={{0,8},{8,0},{16,24},{24,16},{1,9},{9,1},{17,25},{25,17},{2,10},{10... | collective-permute-start | bytes 73736 | tf_op jit(solution)/shard_map/ppermute | solution.py:228
  16.5 4.7 %collective-permute-start.1 = (f32[8,768]{1,0:T(8,128)S(1)}, f32[8,768]{1,0:T(8,128)S(1)}, u32[]{:S(2)}, u32[]{:S(2)}) collective-permute-start(f32[8,768]{1,0:T(8,128)S(1)} %add.9), channel_id=1, source_target_pairs={{0,16},{8,24},{16,0},{24,8},{1,17},{9,25},{17,1},{25,9},{2,18},{10... | collective-permute-start | bytes 73736 | tf_op jit(solution)/shard_map/ppermute | solution.py:228
  21.2 3.9 %collective-permute-start.2 = (f32[8,768]{1,0:T(8,128)S(1)}, f32[8,768]{1,0:T(8,128)S(1)}, u32[]{:S(2)}, u32[]{:S(2)}) collective-permute-start(f32[8,768]{1,0:T(8,128)S(1)} %add.10), channel_id=1, source_target_pairs={{0,2},{2,0},{4,6},{6,4},{1,3},{3,1},{5,7},{7,5},{8,10},{10,8},{12,... | collective-permute-start | bytes 73736 | tf_op jit(solution)/shard_map/ppermute | solution.py:228
  25.1 4.8 %collective-permute-start.3 = (f32[8,768]{1,0:T(8,128)S(1)}, f32[8,768]{1,0:T(8,128)S(1)}, u32[]{:S(2)}, u32[]{:S(2)}) collective-permute-start(f32[8,768]{1,0:T(8,128)S(1)} %add.11.mine), channel_id=1, source_target_pairs={{0,4},{2,6},{4,0},{6,2},{1,5},{3,7},{5,1},{7,3},{8,12},{10,14},{12... | collective-permute-start | bytes 73736 | tf_op jit(solution)/shard_map/ppermute | solution.py:228

commit v2 on v1

--- a/solution.py
+++ b/solution.py
@@ -132,8 +132,8 @@
 
 
 def project_kernel(
-    n_gy, levels, owner, cutoff, relax, era, field_hbm, fy_hbm, fx_hbm, iy_hbm, ix_hbm,
-    share, field, iy, ix, store, fy, fx, bands, field_sem, table_sem,
+    n_gy, levels, owner_hbm, cutoff_hbm, relax_hbm, era_hbm, field_hbm, fy_hbm, fx_hbm, iy_hbm, ix_hbm,
+    share, field, iy, ix, owner, cutoff, relax, era, store, fy, fx, bands, field_sem, small_sem, table_sem,
 ):
     gx, gy = lax.axis_index("gx"), lax.axis_index("gy")
     tables = [
@@ -142,6 +142,14 @@
             ((fy_hbm.at[gy], fy), (fx_hbm.at[gx], fx), (iy_hbm.at[gy], iy), (ix_hbm.at[gx], ix))
         )
     ]
+    small = [
+        pltpu.make_async_copy(src, dst, small_sem.at[n])
+        for n, (src, dst) in enumerate(
+            ((era_hbm, era), (owner_hbm, owner), (cutoff_hbm, cutoff), (relax_hbm, relax))
+        )
+    ]
+    for copy in small:
+        copy.start()
     tables[0].start()
     for f in range(F):
         pltpu.make_async_copy(field_hbm.at[f // levels, f % levels], field.at[f], field_sem.at[f]).start()
@@ -149,6 +157,8 @@
         copy.start()
 
     store[...] = jnp.zeros_like(store)
+    for copy in small:
+        copy.wait()
     for var in range(F // levels):
         store[var * levels : (var + 1) * levels, : 2 * NK * NK] = era[0, var]
     analysis = pack(analysis_rows(store[...]))
@@ -224,6 +234,10 @@
     lax.fori_loop(0, F * steps, end, 0)
 
 
+def in_hbm(value):
+    return pltpu.with_memory_space_constraint(jnp.asarray(value), pltpu.HBM)
+
+
 def swap(value, axis, size, bit):
     return lax.ppermute(value, axis, [(i, i ^ bit) for i in range(size)])
 
@@ -232,9 +246,8 @@
     nvar, levels, ny, nx = model_state.shape
     fy, fx = forward_tables(n_gx, n_gy)
     iy, ix = inverse_tables(n_gx, n_gy)
-    smem = pl.BlockSpec(memory_space=pltpu.SMEM)
     vmem = pl.BlockSpec(memory_space=pltpu.VMEM)
-    hbm = pl.BlockSpec(memory_space=pl.ANY)
+    hbm = pl.BlockSpec(memory_space=pltpu.HBM)
     share, field, iy, ix = pl.pallas_call(
         functools.partial(project_kernel, n_gy, levels),
         out_shape=(
@@ -243,19 +256,24 @@
             pltpu.VMEM((ny, 128), jnp.bfloat16),
             pltpu.VMEM((256, nx), jnp.bfloat16),
         ),
-        in_specs=[smem, smem, smem, vmem, hbm, hbm, hbm, hbm, hbm],
+        in_specs=[hbm] * 9,
         out_specs=[vmem] * 4,
         scratch_shapes=[
+            pltpu.SMEM(owner_map.shape, jnp.int32),
+            pltpu.SMEM(cutoff.shape, jnp.int32),
+            pltpu.SMEM(relax_rate.shape, jnp.float32),
+            pltpu.VMEM(era_store.shape, jnp.float32),
             pltpu.VMEM((F, 1024), jnp.float32),
             pltpu.VMEM((64, ny), jnp.bfloat16),
             pltpu.VMEM((nx, 256), jnp.bfloat16),
             pltpu.VMEM((nx // 128, SLOTS * F, 128), jnp.float32),
             pltpu.SemaphoreType.DMA((F,)),
             pltpu.SemaphoreType.DMA((4,)),
+            pltpu.SemaphoreType.DMA((4,)),
         ],
         compiler_params=pltpu.CompilerParams(vmem_limit_bytes=20 * 2**20),
         name="project",
-    )(owner_map, cutoff, relax_rate, era_store, model_state, fy, fx, iy, ix)
+    )(*(in_hbm(value) for value in (owner_map, cutoff, relax_rate, era_store, model_state, fy, fx, iy, ix)))
 
     steps = [("gx", n_gx, 1 << bit) for bit in range(n_gx.bit_length() - 1)]
     steps += [("gy", n_gy, 1 << bit) for bit in range(n_gy.bit_length() - 1)]

time: 34.3 us -> 24.4 us (0.71)
  local copies, waits for them, and re-layouts: 10.6 us -> 0 us
  Pallas kernels: 8.5 us -> 9.51 us
    unnamed x18 -> x0, local copies, waits for them, and re-layouts: 10.6 us -> none
    pallas_call x1, Pallas kernels: 4.57 us -> 5.59 us  [body(): pl.pallas_call(functools.partial(project_kernel, n_gy, levels), out_shape...]
where the time goes in v2:
time: 24.4 us; the launch traced here: 24.3 us
  Pallas kernels  9.51 us (39%)
  starting transfers between devices  8.49 us (35%)
  waiting for transfers between devices  6.26 us (26%)
    ppermute x4, starting transfers between devices, swap(): return lax.ppermute(value, axis, [(i, i ^ bit) for i in range(size)])  8.49 us
    ppermute x4, waiting for transfers between devices, swap(): return lax.ppermute(value, axis, [(i, i ^ bit) for i in range(size)])  6.26 us
    pallas_call x1, Pallas kernels, body(): pl.pallas_call(functools.partial(project_kernel, n_gy, levels), out_shape...  5.59 us
    pallas_call x1, Pallas kernels, body(): pl.pallas_call(functools.partial(nudge_kernel, levels, chunk), out_shape=...  3.93 us
  transfers between devices with their start and end apart: 4, of which 4 were waited for; matrix products, arithmetic and copies ran while one was open for 0% of the time, Pallas kernels for 0%

profile of v2, /device:TPU:0, one launch (start us, length us, event | category | flops | bytes accessed | tf_op | source)
XLA Modules:
  0.0 24.3 jit_solution(13395819113912825508)
XLA Ops:
  0.0 5.6 %project.1 = (f32[8,768]{1,0:T(8,128)S(1)}, f32[8,512,512]{2,1,0:T(8,128)S(1)}, bf16[512,128]{1,0:T(8,128)(2,1)S(1)}, bf16[256,512]{1,0:T(8,128)(2,1)S(1)}) custom-call(s32[1,2]{1,0:T(1,128)} %owner_hbm.1, s32[2,4]{1,0:T(2,128)} %cutoff_hbm.1, f32[2,4]{1,0:T(2,128)} %relax_hbm.1, f32[1,2,4,882]{3,2,1,0:T(4,128)} %era_hbm.1, f32[2,4,512,512]{3,2,1,0:T(8,128)} %field_hbm.1, ...), custom_call_target="tpu_custom_call" | custom-call | tf_op jit(solution)/shard_map/project/pallas_call | solution.py:251
  5.6 0.5 %collective-permute-start = (f32[8,768]{1,0:T(8,128)S(1)}, f32[8,768]{1,0:T(8,128)S(1)}, u32[]{:S(2)}, u32[]{:S(2)}) collective-permute-start(f32[8,768]{1,0:T(8,128)S(1)} %get-tuple-element.9), channel_id=1, source_target_pairs={{0,8},{8,0},{16,24},{24,16},{1,9},{9,1},{17,25},{25,17},{2,10},{10... | collective-permute-start | bytes 73736 | tf_op jit(solution)/shard_map/ppermute | solution.py:242
  6.1 0.8 %collective-permute-done = f32[8,768]{1,0:T(8,128)S(1)} collective-permute-done((f32[8,768]{1,0:T(8,128)S(1)}, f32[8,768]{1,0:T(8,128)S(1)}, u32[]{:S(2)}, u32[]{:S(2)}) %collective-permute-start) | collective-permute-done | bytes 24608 | tf_op jit(solution)/shard_map/ppermute | solution.py:242
  7.0 2.9 %collective-permute-start.1 = (f32[8,768]{1,0:T(8,128)S(1)}, f32[8,768]{1,0:T(8,128)S(1)}, u32[]{:S(2)}, u32[]{:S(2)}) collective-permute-start(f32[8,768]{1,0:T(8,128)S(1)} %add.9), channel_id=1, source_target_pairs={{0,16},{8,24},{16,0},{24,8},{1,17},{9,25},{17,1},{25,9},{2,18},{10... | collective-permute-start | bytes 73736 | tf_op jit(solution)/shard_map/ppermute | solution.py:242
  9.8 1.8 %collective-permute-done.1 = f32[8,768]{1,0:T(8,128)S(1)} collective-permute-done((f32[8,768]{1,0:T(8,128)S(1)}, f32[8,768]{1,0:T(8,128)S(1)}, u32[]{:S(2)}, u32[]{:S(2)}) %collective-permute-start.1) | collective-permute-done | bytes 24608 | tf_op jit(solution)/shard_map/ppermute | solution.py:242
  11.6 2.1 %collective-permute-start.2 = (f32[8,768]{1,0:T(8,128)S(1)}, f32[8,768]{1,0:T(8,128)S(1)}, u32[]{:S(2)}, u32[]{:S(2)}) collective-permute-start(f32[8,768]{1,0:T(8,128)S(1)} %add.10), channel_id=1, source_target_pairs={{0,2},{2,0},{4,6},{6,4},{1,3},{3,1},{5,7},{7,5},{8,10},{10,8},{12,... | collective-permute-start | bytes 73736 | tf_op jit(solution)/shard_map/ppermute | solution.py:242
  13.7 1.8 %collective-permute-done.2 = f32[8,768]{1,0:T(8,128)S(1)} collective-permute-done((f32[8,768]{1,0:T(8,128)S(1)}, f32[8,768]{1,0:T(8,128)S(1)}, u32[]{:S(2)}, u32[]{:S(2)}) %collective-permute-start.2) | collective-permute-done | bytes 24608 | tf_op jit(solution)/shard_map/ppermute | solution.py:242
  15.5 3.0 %collective-permute-start.3 = (f32[8,768]{1,0:T(8,128)S(1)}, f32[8,768]{1,0:T(8,128)S(1)}, u32[]{:S(2)}, u32[]{:S(2)}) collective-permute-start(f32[8,768]{1,0:T(8,128)S(1)} %add.11.mine), channel_id=1, source_target_pairs={{0,4},{2,6},{4,0},{6,2},{1,5},{3,7},{5,1},{7,3},{8,12},{10,14},{12... | collective-permute-start | bytes 73736 | tf_op jit(solution)/shard_map/ppermute | solution.py:242
  18.6 1.8 %collective-permute-done.3.other = f32[8,768]{1,0:T(8,128)S(1)} collective-permute-done((f32[8,768]{1,0:T(8,128)S(1)}, f32[8,768]{1,0:T(8,128)S(1)}, u32[]{:S(2)}, u32[]{:S(2)}) %collective-permute-start.3) | collective-permute-done | bytes 24608 | tf_op jit(solution)/shard_map/ppermute | solution.py:242
  20.4 3.9 %nudge.1 = f32[2,4,512,512]{3,2,1,0:T(8,128)} custom-call(f32[8,768]{1,0:T(8,128)S(1)} %add.11.mine, f32[8,768]{1,0:T(8,128)S(1)} %collective-permute-done.3.other, f32[8,512,512]{2,1,0:T(8,128)S(1)} %get-tuple-element.10.field, bf16[512,128]{1,0:T(8,128)(2,1)S(1)} %get-tuple-element.11.iy, bf16[256,512]{1,0:T(8,128)(2,1)S(1)} %get-tuple-element.12.ix), custom_call_target="tpu_custom_call" | custom-call | tf_op jit(solution)/shard_map/nudge/pallas_call | solution.py:285
  (3 shorter events, 0.0 us)
Async XLA Ops:
  5.6 1.4 %collective-permute-start = (f32[8,768]{1,0:T(8,128)S(1)}, f32[8,768]{1,0:T(8,128)S(1)}, u32[]{:S(2)}, u32[]{:S(2)}) collective-permute-start(f32[8,768]{1,0:T(8,128)S(1)} %get-tuple-element.9), channel_id=1, source_target_pairs={{0,8},{8,0},{16,24},{24,16},{1,9},{9,1},{17,25},{25,17},{2,10},{10... | collective-permute-start | bytes 73736 | tf_op jit(solution)/shard_map/ppermute | solution.py:242
  7.0 4.7 %collective-permute-start.1 = (f32[8,768]{1,0:T(8,128)S(1)}, f32[8,768]{1,0:T(8,128)S(1)}, u32[]{:S(2)}, u32[]{:S(2)}) collective-permute-start(f32[8,768]{1,0:T(8,128)S(1)} %add.9), channel_id=1, source_target_pairs={{0,16},{8,24},{16,0},{24,8},{1,17},{9,25},{17,1},{25,9},{2,18},{10... | collective-permute-start | bytes 73736 | tf_op jit(solution)/shard_map/ppermute | solution.py:242
  11.6 3.9 %collective-permute-start.2 = (f32[8,768]{1,0:T(8,128)S(1)}, f32[8,768]{1,0:T(8,128)S(1)}, u32[]{:S(2)}, u32[]{:S(2)}) collective-permute-start(f32[8,768]{1,0:T(8,128)S(1)} %add.10), channel_id=1, source_target_pairs={{0,2},{2,0},{4,6},{6,4},{1,3},{3,1},{5,7},{7,5},{8,10},{10,8},{12,... | collective-permute-start | bytes 73736 | tf_op jit(solution)/shard_map/ppermute | solution.py:242
  15.5 4.8 %collective-permute-start.3 = (f32[8,768]{1,0:T(8,128)S(1)}, f32[8,768]{1,0:T(8,128)S(1)}, u32[]{:S(2)}, u32[]{:S(2)}) collective-permute-start(f32[8,768]{1,0:T(8,128)S(1)} %add.11.mine), channel_id=1, source_target_pairs={{0,4},{2,6},{4,0},{6,2},{1,5},{3,7},{5,1},{7,3},{8,12},{10,14},{12... | collective-permute-start | bytes 73736 | tf_op jit(solution)/shard_map/ppermute | solution.py:242

commit v3 on v2

--- a/solution.py
+++ b/solution.py
@@ -151,8 +151,12 @@
     for copy in small:
         copy.start()
     tables[0].start()
-    for f in range(F):
-        pltpu.make_async_copy(field_hbm.at[f // levels, f % levels], field.at[f], field_sem.at[f]).start()
+    window = 4
+    for f, pieces in enumerate((1, 1, 1, 1)):
+        rows = field.shape[1] // pieces
+        for piece in range(pieces):
+            at = pl.ds(piece * rows, rows)
+            pltpu.make_async_copy(field_hbm.at[f // levels, f % levels, at], field.at[f, at], field_sem.at[f]).start()
     for copy in tables[1:]:
         copy.start()
 
@@ -177,6 +181,12 @@
 
     def one(f, _):
         pltpu.make_async_copy(field_hbm.at[0, 0], field.at[f], field_sem.at[f]).wait()
+
+        @pl.when(f + window < F)
+        def _():
+            n = f + window
+            pltpu.make_async_copy(field_hbm.at[n // levels, n % levels], field.at[n], field_sem.at[n]).start()
+
         high, low = split(field[f])
         wide = dot(fy[...], high)
         band = wide[:SLOTS] + wide[32 : 32 + SLOTS] + dot(fy[:32], low)[:SLOTS]

time: 24.4 us -> 23.4 us (0.959)
  Pallas kernels: 9.51 us -> 8.49 us
    pallas_call x1, Pallas kernels: 5.59 us -> 4.56 us  [body(): pl.pallas_call(functools.partial(project_kernel, n_gy, levels), out_shape...]
where the time goes in v3:
time: 23.4 us; the launch traced here: 23.3 us
  starting transfers between devices  8.5 us (36%)
  Pallas kernels  8.49 us (36%)
  waiting for transfers between devices  6.26 us (27%)
    ppermute x4, starting transfers between devices, swap(): return lax.ppermute(value, axis, [(i, i ^ bit) for i in range(size)])  8.5 us
    ppermute x4, waiting for transfers between devices, swap(): return lax.ppermute(value, axis, [(i, i ^ bit) for i in range(size)])  6.26 us
    pallas_call x1, Pallas kernels, body(): pl.pallas_call(functools.partial(project_kernel, n_gy, levels), out_shape...  4.56 us
    pallas_call x1, Pallas kernels, body(): pl.pallas_call(functools.partial(nudge_kernel, levels, chunk), out_shape=...  3.93 us
  transfers between devices with their start and end apart: 4, of which 4 were waited for; matrix products, arithmetic and copies ran while one was open for 0% of the time, Pallas kernels for 0%

profile of v3, /device:TPU:0, one launch (start us, length us, event | category | flops | bytes accessed | tf_op | source)
XLA Modules:
  0.0 23.3 jit_solution(8822627992608691508)
XLA Ops:
  0.0 4.6 %project.1 = (f32[8,768]{1,0:T(8,128)S(1)}, f32[8,512,512]{2,1,0:T(8,128)S(1)}, bf16[512,128]{1,0:T(8,128)(2,1)S(1)}, bf16[256,512]{1,0:T(8,128)(2,1)S(1)}) custom-call(s32[1,2]{1,0:T(1,128)} %owner_hbm.1, s32[2,4]{1,0:T(2,128)} %cutoff_hbm.1, f32[2,4]{1,0:T(2,128)} %relax_hbm.1, f32[1,2,4,882]{3,2,1,0:T(4,128)} %era_hbm.1, f32[2,4,512,512]{3,2,1,0:T(8,128)} %field_hbm.1, ...), custom_call_target="tpu_custom_call" | custom-call | tf_op jit(solution)/shard_map/project/pallas_call | solution.py:261
  4.6 0.5 %collective-permute-start = (f32[8,768]{1,0:T(8,128)S(1)}, f32[8,768]{1,0:T(8,128)S(1)}, u32[]{:S(2)}, u32[]{:S(2)}) collective-permute-start(f32[8,768]{1,0:T(8,128)S(1)} %get-tuple-element.9), channel_id=1, source_target_pairs={{0,8},{8,0},{16,24},{24,16},{1,9},{9,1},{17,25},{25,17},{2,10},{10... | collective-permute-start | bytes 73736 | tf_op jit(solution)/shard_map/ppermute | solution.py:252
  5.1 0.8 %collective-permute-done = f32[8,768]{1,0:T(8,128)S(1)} collective-permute-done((f32[8,768]{1,0:T(8,128)S(1)}, f32[8,768]{1,0:T(8,128)S(1)}, u32[]{:S(2)}, u32[]{:S(2)}) %collective-permute-start) | collective-permute-done | bytes 24608 | tf_op jit(solution)/shard_map/ppermute | solution.py:252
  5.9 2.9 %collective-permute-start.1 = (f32[8,768]{1,0:T(8,128)S(1)}, f32[8,768]{1,0:T(8,128)S(1)}, u32[]{:S(2)}, u32[]{:S(2)}) collective-permute-start(f32[8,768]{1,0:T(8,128)S(1)} %add.9), channel_id=1, source_target_pairs={{0,16},{8,24},{16,0},{24,8},{1,17},{9,25},{17,1},{25,9},{2,18},{10... | collective-permute-start | bytes 73736 | tf_op jit(solution)/shard_map/ppermute | solution.py:252
  8.8 1.8 %collective-permute-done.1 = f32[8,768]{1,0:T(8,128)S(1)} collective-permute-done((f32[8,768]{1,0:T(8,128)S(1)}, f32[8,768]{1,0:T(8,128)S(1)}, u32[]{:S(2)}, u32[]{:S(2)}) %collective-permute-start.1) | collective-permute-done | bytes 24608 | tf_op jit(solution)/shard_map/ppermute | solution.py:252
  10.6 2.1 %collective-permute-start.2 = (f32[8,768]{1,0:T(8,128)S(1)}, f32[8,768]{1,0:T(8,128)S(1)}, u32[]{:S(2)}, u32[]{:S(2)}) collective-permute-start(f32[8,768]{1,0:T(8,128)S(1)} %add.10), channel_id=1, source_target_pairs={{0,2},{2,0},{4,6},{6,4},{1,3},{3,1},{5,7},{7,5},{8,10},{10,8},{12,... | collective-permute-start | bytes 73736 | tf_op jit(solution)/shard_map/ppermute | solution.py:252
  12.7 1.8 %collective-permute-done.2 = f32[8,768]{1,0:T(8,128)S(1)} collective-permute-done((f32[8,768]{1,0:T(8,128)S(1)}, f32[8,768]{1,0:T(8,128)S(1)}, u32[]{:S(2)}, u32[]{:S(2)}) %collective-permute-start.2) | collective-permute-done | bytes 24608 | tf_op jit(solution)/shard_map/ppermute | solution.py:252
  14.5 3.0 %collective-permute-start.3 = (f32[8,768]{1,0:T(8,128)S(1)}, f32[8,768]{1,0:T(8,128)S(1)}, u32[]{:S(2)}, u32[]{:S(2)}) collective-permute-start(f32[8,768]{1,0:T(8,128)S(1)} %add.11.mine), channel_id=1, source_target_pairs={{0,4},{2,6},{4,0},{6,2},{1,5},{3,7},{5,1},{7,3},{8,12},{10,14},{12... | collective-permute-start | bytes 73736 | tf_op jit(solution)/shard_map/ppermute | solution.py:252
  17.5 1.8 %collective-permute-done.3.other = f32[8,768]{1,0:T(8,128)S(1)} collective-permute-done((f32[8,768]{1,0:T(8,128)S(1)}, f32[8,768]{1,0:T(8,128)S(1)}, u32[]{:S(2)}, u32[]{:S(2)}) %collective-permute-start.3) | collective-permute-done | bytes 24608 | tf_op jit(solution)/shard_map/ppermute | solution.py:252
  19.3 3.9 %nudge.1 = f32[2,4,512,512]{3,2,1,0:T(8,128)} custom-call(f32[8,768]{1,0:T(8,128)S(1)} %add.11.mine, f32[8,768]{1,0:T(8,128)S(1)} %collective-permute-done.3.other, f32[8,512,512]{2,1,0:T(8,128)S(1)} %get-tuple-element.10.field, bf16[512,128]{1,0:T(8,128)(2,1)S(1)} %get-tuple-element.11.iy, bf16[256,512]{1,0:T(8,128)(2,1)S(1)} %get-tuple-element.12.ix), custom_call_target="tpu_custom_call" | custom-call | tf_op jit(solution)/shard_map/nudge/pallas_call | solution.py:295
  (3 shorter events, 0.0 us)
Async XLA Ops:
  4.6 1.4 %collective-permute-start = (f32[8,768]{1,0:T(8,128)S(1)}, f32[8,768]{1,0:T(8,128)S(1)}, u32[]{:S(2)}, u32[]{:S(2)}) collective-permute-start(f32[8,768]{1,0:T(8,128)S(1)} %get-tuple-element.9), channel_id=1, source_target_pairs={{0,8},{8,0},{16,24},{24,16},{1,9},{9,1},{17,25},{25,17},{2,10},{10... | collective-permute-start | bytes 73736 | tf_op jit(solution)/shard_map/ppermute | solution.py:252
  5.9 4.7 %collective-permute-start.1 = (f32[8,768]{1,0:T(8,128)S(1)}, f32[8,768]{1,0:T(8,128)S(1)}, u32[]{:S(2)}, u32[]{:S(2)}) collective-permute-start(f32[8,768]{1,0:T(8,128)S(1)} %add.9), channel_id=1, source_target_pairs={{0,16},{8,24},{16,0},{24,8},{1,17},{9,25},{17,1},{25,9},{2,18},{10... | collective-permute-start | bytes 73736 | tf_op jit(solution)/shard_map/ppermute | solution.py:252
  10.6 3.9 %collective-permute-start.2 = (f32[8,768]{1,0:T(8,128)S(1)}, f32[8,768]{1,0:T(8,128)S(1)}, u32[]{:S(2)}, u32[]{:S(2)}) collective-permute-start(f32[8,768]{1,0:T(8,128)S(1)} %add.10), channel_id=1, source_target_pairs={{0,2},{2,0},{4,6},{6,4},{1,3},{3,1},{5,7},{7,5},{8,10},{10,8},{12,... | collective-permute-start | bytes 73736 | tf_op jit(solution)/shard_map/ppermute | solution.py:252
  14.5 4.8 %collective-permute-start.3 = (f32[8,768]{1,0:T(8,128)S(1)}, f32[8,768]{1,0:T(8,128)S(1)}, u32[]{:S(2)}, u32[]{:S(2)}) collective-permute-start(f32[8,768]{1,0:T(8,128)S(1)} %add.11.mine), channel_id=1, source_target_pairs={{0,4},{2,6},{4,0},{6,2},{1,5},{3,7},{5,1},{7,3},{8,12},{10,14},{12... | collective-permute-start | bytes 73736 | tf_op jit(solution)/shard_map/ppermute | solution.py:252

commit v4 on v2

--- a/solution.py
+++ b/solution.py
@@ -151,8 +151,11 @@
     for copy in small:
         copy.start()
     tables[0].start()
-    for f in range(F):
+    def load(f, _):
         pltpu.make_async_copy(field_hbm.at[f // levels, f % levels], field.at[f], field_sem.at[f]).start()
+        return 0
+
+    lax.fori_loop(0, F, load, 0)
     for copy in tables[1:]:
         copy.start()
 
@@ -177,6 +180,7 @@
 
     def one(f, _):
         pltpu.make_async_copy(field_hbm.at[0, 0], field.at[f], field_sem.at[f]).wait()
+
         high, low = split(field[f])
         wide = dot(fy[...], high)
         band = wide[:SLOTS] + wide[32 : 32 + SLOTS] + dot(fy[:32], low)[:SLOTS]
@@ -238,8 +242,15 @@
     return pltpu.with_memory_space_constraint(jnp.asarray(value), pltpu.HBM)
 
 
-def swap(value, axis, size, bit):
-    return lax.ppermute(value, axis, [(i, i ^ bit) for i in range(size)])
+def phases_of(n_gx, n_gy):
+    along_y = [[1 << bit] for bit in range(n_gy.bit_length() - 1)]
+    along_x = [[bits * n_gy for bits in range(1, min(n_gx, 4))]]
+    along_x += [[n_gy << bit] for bit in range(2, n_gx.bit_length() - 1)]
+    return along_y[:1] + along_x + along_y[1:]
+
+
+def swap(value, size, bits):
+    return lax.ppermute(value, ("gx", "gy"), [(i, i ^ bits) for i in range(size)])
 
 
 def body(n_gx, n_gy, model_state, cutoff, relax_rate, owner_map, era_store):
@@ -275,11 +286,12 @@
         name="project",
     )(*(in_hbm(value) for value in (owner_map, cutoff, relax_rate, era_store, model_state, fy, fx, iy, ix)))
 
-    steps = [("gx", n_gx, 1 << bit) for bit in range(n_gx.bit_length() - 1)]
-    steps += [("gy", n_gy, 1 << bit) for bit in range(n_gy.bit_length() - 1)]
-    for step in steps[:-1]:
-        share = share + swap(share, *step)
-    other = swap(share, *steps[-1])
+    phases = phases_of(n_gx, n_gy)
+    for phase in phases[:-1]:
+        got = [swap(share, n_gx * n_gy, bits) for bits in phase]
+        for other in got:
+            share = share + other
+    other = sum(swap(share, n_gx * n_gy, bits) for bits in phases[-1])
 
     chunk = min(ny, 256)
     nudged = pl.pallas_call(

time: 24.4 us -> 22.1 us (0.906)
  Pallas kernels: 9.51 us -> 8.11 us
  waiting for transfers between devices: 6.26 us -> 5.69 us
  starting transfers between devices: 8.49 us -> 8.08 us
    pallas_call x1, Pallas kernels: 5.59 us -> 4.18 us  [body(): pl.pallas_call(functools.partial(project_kernel, n_gy, levels), out_shape...]
    ppermute x4 -> x5, waiting for transfers between devices: 6.26 us -> 5.69 us  [swap(): lax.ppermute(value, ('gx', 'gy'), [(i, i ^ bits) for i in range(size)])]
    ppermute x4 -> x5, starting transfers between devices: 8.49 us -> 8.08 us  [swap(): lax.ppermute(value, ('gx', 'gy'), [(i, i ^ bits) for i in range(size)])]
  transfers between devices with their start and end apart: 4 -> 5, of which waited for: 4 -> 4; matrix products, arithmetic and copies ran while one was open for 0% -> 0% of each run, Pallas kernels for 0% -> 0%
where the time goes in v4:
time: 22.1 us; the launch traced here: 21.9 us
  Pallas kernels  8.11 us (37%)
  starting transfers between devices  8.08 us (37%)
  waiting for transfers between devices  5.69 us (26%)
    ppermute x5, starting transfers between devices, swap(): lax.ppermute(value, ('gx', 'gy'), [(i, i ^ bits) for i in range(size)])  8.08 us
    ppermute x5, waiting for transfers between devices, swap(): lax.ppermute(value, ('gx', 'gy'), [(i, i ^ bits) for i in range(size)])  5.69 us
    pallas_call x1, Pallas kernels, body(): pl.pallas_call(functools.partial(project_kernel, n_gy, levels), out_shape...  4.18 us
    pallas_call x1, Pallas kernels, body(): pl.pallas_call(functools.partial(nudge_kernel, levels, chunk), out_shape=...  3.93 us
  transfers between devices with their start and end apart: 5, of which 4 were waited for; matrix products, arithmetic and copies ran while one was open for 0% of the time, Pallas kernels for 0%

profile of v4, /device:TPU:0, one launch (start us, length us, event | category | flops | bytes accessed | tf_op | source)
XLA Modules:
  0.0 21.9 jit_solution(18322560957840118936)
XLA Ops:
  0.0 4.2 %project.1 = (f32[8,768]{1,0:T(8,128)S(1)}, f32[8,512,512]{2,1,0:T(8,128)S(1)}, bf16[512,128]{1,0:T(8,128)(2,1)S(1)}, bf16[256,512]{1,0:T(8,128)(2,1)S(1)}) custom-call(s32[1,2]{1,0:T(1,128)} %owner_hbm.1, s32[2,4]{1,0:T(2,128)} %cutoff_hbm.1, f32[2,4]{1,0:T(2,128)} %relax_hbm.1, f32[1,2,4,882]{3,2,1,0:T(4,128)} %era_hbm.1, f32[2,4,512,512]{3,2,1,0:T(8,128)} %field_hbm.1, ...), custom_call_target="tpu_custom_call" | custom-call | tf_op jit(solution)/shard_map/project/pallas_call | solution.py:262
  4.2 3.1 %collective-permute-start = (f32[8,768]{1,0:T(8,128)S(1)}, f32[8,768]{1,0:T(8,128)S(1)}, u32[]{:S(2)}, u32[]{:S(2)}) collective-permute-start(f32[8,768]{1,0:T(8,128)S(1)} %get-tuple-element.9), channel_id=1, source_target_pairs={{0,2},{2,0},{4,6},{6,4},{8,10},{10,8},{12,14},{14,12},{16,18},{18,... | collective-permute-start | bytes 73736 | tf_op jit(solution)/shard_map/ppermute | solution.py:253
  7.3 1.8 %collective-permute-done = f32[8,768]{1,0:T(8,128)S(1)} collective-permute-done((f32[8,768]{1,0:T(8,128)S(1)}, f32[8,768]{1,0:T(8,128)S(1)}, u32[]{:S(2)}, u32[]{:S(2)}) %collective-permute-start) | collective-permute-done | bytes 24608 | tf_op jit(solution)/shard_map/ppermute | solution.py:253
  9.1 0.3 %collective-permute-start.3 = (f32[8,768]{1,0:T(8,128)S(1)}, f32[8,768]{1,0:T(8,128)S(1)}, u32[]{:S(2)}, u32[]{:S(2)}) collective-permute-start(f32[8,768]{1,0:T(8,128)S(1)} %add.12), channel_id=1, source_target_pairs={{0,24},{2,26},{4,28},{6,30},{8,16},{10,18},{12,20},{14,22},{16,8},... | collective-permute-start | bytes 73736 | tf_op jit(solution)/shard_map/ppermute | solution.py:253
  9.3 1.8 %collective-permute-start.2 = (f32[8,768]{1,0:T(8,128)S(1)}, f32[8,768]{1,0:T(8,128)S(1)}, u32[]{:S(2)}, u32[]{:S(2)}) collective-permute-start(f32[8,768]{1,0:T(8,128)S(1)} %add.12), channel_id=1, source_target_pairs={{0,16},{2,18},{4,20},{6,22},{8,24},{10,26},{12,28},{14,30},{16,0},... | collective-permute-start | bytes 73736 | tf_op jit(solution)/shard_map/ppermute | solution.py:253
  11.1 0.0 collective-permute-start.1
  11.2 1.2 %collective-permute-done.3 = f32[8,768]{1,0:T(8,128)S(1)} collective-permute-done((f32[8,768]{1,0:T(8,128)S(1)}, f32[8,768]{1,0:T(8,128)S(1)}, u32[]{:S(2)}, u32[]{:S(2)}) %collective-permute-start.3) | collective-permute-done | bytes 24608 | tf_op jit(solution)/shard_map/ppermute | solution.py:253
  12.3 0.8 %collective-permute-done.2 = f32[8,768]{1,0:T(8,128)S(1)} collective-permute-done((f32[8,768]{1,0:T(8,128)S(1)}, f32[8,768]{1,0:T(8,128)S(1)}, u32[]{:S(2)}, u32[]{:S(2)}) %collective-permute-start.2) | collective-permute-done | bytes 24608 | tf_op jit(solution)/shard_map/ppermute | solution.py:253
  13.2 0.0 collective-permute-done.1
  13.2 2.9 %collective-permute-start.4 = (f32[8,768]{1,0:T(8,128)S(1)}, f32[8,768]{1,0:T(8,128)S(1)}, u32[]{:S(2)}, u32[]{:S(2)}) collective-permute-start(f32[8,768]{1,0:T(8,128)S(1)} %add_add_fusion.mine), channel_id=1, source_target_pairs={{0,4},{2,6},{4,0},{6,2},{8,12},{10,14},{12,8},{14,10},{16,20},{18,... | collective-permute-start | bytes 73736 | tf_op jit(solution)/shard_map/ppermute | solution.py:253
  16.1 1.9 %collective-permute-done.4.other = f32[8,768]{1,0:T(8,128)S(1)} collective-permute-done((f32[8,768]{1,0:T(8,128)S(1)}, f32[8,768]{1,0:T(8,128)S(1)}, u32[]{:S(2)}, u32[]{:S(2)}) %collective-permute-start.4) | collective-permute-done | bytes 24608 | tf_op jit(solution)/shard_map/ppermute | solution.py:253
  18.0 3.9 %nudge.1 = f32[2,4,512,512]{3,2,1,0:T(8,128)} custom-call(f32[8,768]{1,0:T(8,128)S(1)} %add_add_fusion.mine, f32[8,768]{1,0:T(8,128)S(1)} %collective-permute-done.4.other, f32[8,512,512]{2,1,0:T(8,128)S(1)} %get-tuple-element.10.field, bf16[512,128]{1,0:T(8,128)(2,1)S(1)} %get-tuple-element.11.iy, bf16[256,512]{1,0:T(8,128)(2,1)S(1)} %get-tuple-element.12.ix), custom_call_target="tpu_custom_call" | custom-call | tf_op jit(solution)/shard_map/nudge/pallas_call | solution.py:297
  (2 shorter events, 0.0 us)
Async XLA Ops:
  4.2 4.9 %collective-permute-start = (f32[8,768]{1,0:T(8,128)S(1)}, f32[8,768]{1,0:T(8,128)S(1)}, u32[]{:S(2)}, u32[]{:S(2)}) collective-permute-start(f32[8,768]{1,0:T(8,128)S(1)} %get-tuple-element.9), channel_id=1, source_target_pairs={{0,2},{2,0},{4,6},{6,4},{8,10},{10,8},{12,14},{14,12},{16,18},{18,... | collective-permute-start | bytes 73736 | tf_op jit(solution)/shard_map/ppermute | solution.py:253
  9.1 3.3 %collective-permute-start.3 = (f32[8,768]{1,0:T(8,128)S(1)}, f32[8,768]{1,0:T(8,128)S(1)}, u32[]{:S(2)}, u32[]{:S(2)}) collective-permute-start(f32[8,768]{1,0:T(8,128)S(1)} %add.12), channel_id=1, source_target_pairs={{0,24},{2,26},{4,28},{6,30},{8,16},{10,18},{12,20},{14,22},{16,8},... | collective-permute-start | bytes 73736 | tf_op jit(solution)/shard_map/ppermute | solution.py:253
  9.3 3.8 %collective-permute-start.2 = (f32[8,768]{1,0:T(8,128)S(1)}, f32[8,768]{1,0:T(8,128)S(1)}, u32[]{:S(2)}, u32[]{:S(2)}) collective-permute-start(f32[8,768]{1,0:T(8,128)S(1)} %add.12), channel_id=1, source_target_pairs={{0,16},{2,18},{4,20},{6,22},{8,24},{10,26},{12,28},{14,30},{16,0},... | collective-permute-start | bytes 73736 | tf_op jit(solution)/shard_map/ppermute | solution.py:253
  11.1 2.1 %collective-permute-start.1 = (f32[8,768]{1,0:T(8,128)S(1)}, f32[8,768]{1,0:T(8,128)S(1)}, u32[]{:S(2)}, u32[]{:S(2)}) collective-permute-start(f32[8,768]{1,0:T(8,128)S(1)} %add.12), channel_id=1, source_target_pairs={{0,8},{2,10},{4,12},{6,14},{8,0},{10,2},{12,4},{14,6},{16,24},{18,... | collective-permute-start | bytes 73736 | tf_op jit(solution)/shard_map/ppermute | solution.py:253
  13.2 4.8 %collective-permute-start.4 = (f32[8,768]{1,0:T(8,128)S(1)}, f32[8,768]{1,0:T(8,128)S(1)}, u32[]{:S(2)}, u32[]{:S(2)}) collective-permute-start(f32[8,768]{1,0:T(8,128)S(1)} %add_add_fusion.mine), channel_id=1, source_target_pairs={{0,4},{2,6},{4,0},{6,2},{8,12},{10,14},{12,8},{14,10},{16,20},{18,... | collective-permute-start | bytes 73736 | tf_op jit(solution)/shard_map/ppermute | solution.py:253

commit v5 on v4

--- a/solution.py
+++ b/solution.py
@@ -15,20 +15,31 @@
 NK = 21
 F = 8
 GROUP = 32
+FRONT = 16
 SLOTS = 24
-PACKED = SLOTS * GROUP
+PACKED = FRONT * GROUP
+BACK_FROM = {1: 19, 2: 23, 3: 23, 4: 31, 5: 31}
 
 
 def basis(positions, length):
-    wave = np.concatenate([np.arange(KC + 1), np.arange(1, KC + 1)])
-    angle = np.mod(positions[:, None] * wave[None, :], length) * (2 * np.pi / length)
-    return np.where(np.arange(NK) <= KC, np.cos(angle), np.sin(angle))
+    order = np.arange(NK)
+    angle = np.mod(positions[:, None] * ((order + 1) // 2)[None, :], length) * (2 * np.pi / length)
+    return np.where((order == 0) | (order % 2 == 1), np.cos(angle), np.sin(angle))
 
 
 def halves(table):
     high = table.astype(ml_dtypes.bfloat16)
     low = (table - high.astype(np.float64)).astype(ml_dtypes.bfloat16)
     return high, low
+
+
+def both_ways(high, low):
+    table = np.zeros((high.shape[0], 8, GROUP), ml_dtypes.bfloat16)
+    for group in range(4):
+        half = low if group % 2 else high
+        table[:, group, :NK] = half
+        table[:, 4 + group, GROUP - NK :] = half[:, ::-1]
+    return table.reshape(-1, 256)
 
 
 def forward_tables(n_gx, n_gy):
@@ -40,11 +51,7 @@
     along_y[:, 32 : 32 + NK] = low.reshape(n_gy, ny, NK).transpose(0, 2, 1)
     high, low = halves(basis(np.arange(NX), NX) * weight / NX)
     nx = NX // n_gx
-    along_x = np.zeros((n_gx, nx, 256), ml_dtypes.bfloat16)
-    for group in range(4):
-        at = group * GROUP
-        along_x[:, :, at : at + NK] = high.reshape(n_gx, nx, NK)
-        along_x[:, :, 128 + at : 128 + at + NK] = low.reshape(n_gx, nx, NK)
+    along_x = both_ways(high, low).reshape(n_gx, nx, 256)
     return along_y, along_x
 
 
@@ -52,18 +59,11 @@
     high, low = halves(basis(np.arange(NY), NY))
     ny = NY // n_gy
     along_y = np.zeros((n_gy, ny, 128), ml_dtypes.bfloat16)
-    for slot in range(NK):
-        at = (slot % 4) * (SLOTS // 4) + slot // 4
-        along_y[:, :, at] = high[:, slot].reshape(n_gy, ny)
-        along_y[:, :, SLOTS + at] = low[:, slot].reshape(n_gy, ny)
-        along_y[:, :, 2 * SLOTS + at] = high[:, slot].reshape(n_gy, ny)
+    for first, half in ((0, high), (SLOTS, low), (2 * SLOTS, high)):
+        along_y[:, :, first : first + NK] = half.reshape(n_gy, ny, NK)
     high, low = halves(basis(np.arange(NX), NX))
     nx = NX // n_gx
-    along_x = np.zeros((n_gx, 256, nx), ml_dtypes.bfloat16)
-    for group in range(4):
-        at = group * GROUP
-        along_x[:, at : at + NK] = high.reshape(n_gx, nx, NK).transpose(0, 2, 1)
-        along_x[:, 128 + at : 128 + at + NK] = low.reshape(n_gx, nx, NK).transpose(0, 2, 1)
+    along_x = both_ways(high, low).reshape(n_gx, nx, 256).transpose(0, 2, 1)
     return along_y, along_x
 
 
@@ -76,8 +76,9 @@
     return jnp.dot(left, right, preferred_element_type=jnp.float32)
 
 
-def lane_group(shape):
-    return lax.broadcasted_iota(jnp.int32, shape, 1) // GROUP
+def lanes_of(shape):
+    lane = lax.broadcasted_iota(jnp.int32, shape, 1)
+    return lane // GROUP, lane % GROUP
 
 
 def analysis_rows(store):
@@ -90,37 +91,65 @@
         window = store[:, base : base + width]
         pieces.append(pltpu.roll(window, (width - off) % width, 1)[:, :128] if off else window[:, :128])
     high, low = split(jnp.concatenate(pieces, axis=0))
-    wave = lax.broadcasted_iota(jnp.int32, (128, 128), 0) - KC
-    column = lax.broadcasted_iota(jnp.int32, (128, 128), 1) % GROUP
-    number = jnp.where(column <= KC, column, column - KC)
+    wave = lax.broadcasted_iota(jnp.int32, (128, 256), 0) - KC
+    group, column = lanes_of((128, 256))
+    column = jnp.where(group < 4, column, GROUP - 1 - column)
+    number = (column + 1) // 2
     plus = jnp.where(wave == number, 1.0, 0.0)
     minus = jnp.where((wave == -number) & (number > 0), 1.0, 0.0)
-    fold = jnp.where(column <= KC, plus + minus, plus - minus)
+    fold = jnp.where(column % 2 == 1, plus + minus, plus - minus)
     fold = jnp.where(column < NK, fold, 0.0).astype(jnp.bfloat16)
     folded = dot(high, fold) + dot(low, fold)
-    part = [folded[8 * row : 8 * row + 8] for row in range(2 * NK)]
-    real, imag = part[:NK], part[NK:]
-    even = lax.broadcasted_iota(jnp.int32, (8, 128), 1) % GROUP <= KC
-    rows = [jnp.where(even, real[KC], -imag[KC])]
-    for wave in range(1, KC + 1):
+    column = lanes_of((8, 128))[1]
+    rows = []
+    for slot in range(NK):
+        wave, back = (slot + 1) // 2, slot >= FRONT
+        lanes = slice(128, 256) if back else slice(0, 128)
+        along = GROUP - 1 - column if back else column
+        even = (along == 0) | (along % 2 == 1)
         up, down = KC + wave, KC - wave
-        rows.append(jnp.where(even, real[up] + real[down], -(imag[up] + imag[down])))
-    for wave in range(1, KC + 1):
-        up, down = KC + wave, KC - wave
-        rows.append(-jnp.where(even, imag[up] - imag[down], real[up] - real[down]))
+        real_up, real_down = (folded[8 * row : 8 * row + 8, lanes] for row in (up, down))
+        imag_up, imag_down = (folded[8 * row : 8 * row + 8, lanes] for row in (NK + up, NK + down))
+        if wave == 0:
+            rows.append(jnp.where(even, real_up, -imag_up))
+        elif slot % 2:
+            rows.append(jnp.where(even, real_up + real_down, -(imag_up + imag_down)))
+        else:
+            rows.append(-jnp.where(even, imag_up - imag_down, real_up - real_down))
     return rows
 
 
 def pack(rows):
-    group = lane_group((8, 128))
+    group, column = lanes_of((8, 128))
     blocks = []
-    for block in range(SLOTS // 4):
+    for block in range(FRONT // 4):
         total = jnp.zeros((8, 128), jnp.float32)
         for j in range(4):
-            if 4 * block + j < len(rows):
-                total = jnp.where(group == j, rows[4 * block + j], total)
+            at = 4 * block + j
+            total = jnp.where(group == j, rows[at], total)
+            if at in BACK_FROM:
+                total = jnp.where((group == j) & (column >= BACK_FROM[at]), rows[at + FRONT - 1], total)
         blocks.append(total)
     return jnp.concatenate(blocks, axis=1)
+
+
+def unpack(packed):
+    group, column = lanes_of((8, 128))
+    zero = jnp.zeros((8, 128), jnp.float32)
+    rows = [None] * SLOTS
+    for block in range(FRONT // 4):
+        here = packed[:, 128 * block : 128 * block + 128]
+        after = pltpu.roll(here, GROUP, 1)
+        for j in range(4):
+            at = 4 * block + j
+            row = jnp.where(group == j, here, jnp.where(group == (j + 1) % 4, after, 0.0))
+            if at in BACK_FROM:
+                back = column >= BACK_FROM[at]
+                rows[at + FRONT - 1] = jnp.concatenate([zero, jnp.where(back, row, 0.0)], axis=1)
+                row = jnp.where(back, 0.0, row)
+            rows[at] = jnp.concatenate([row, zero], axis=1)
+    empty = jnp.zeros((8, 256), jnp.float32)
+    return jnp.concatenate([empty if row is None else row for row in rows], axis=0)
 
 
 def per_field(values):
@@ -169,10 +198,13 @@
     mine = per_field([(owner[0, f // levels] == me).astype(jnp.int32) for f in range(F)])
     limit = per_field([cutoff[f // levels, f % levels] for f in range(F)])
     rate = per_field([relax[f // levels, f % levels] for f in range(F)])
-    lane = lax.broadcasted_iota(jnp.int32, (F, PACKED), 1)
-    slot, column = lane // GROUP, lane % GROUP
-    ky = jnp.where(slot <= KC, slot, slot - KC)
-    kx = jnp.where(column <= KC, column, column - KC)
+    group, column = lanes_of((F, PACKED))
+    start = jnp.full((F, PACKED), GROUP)
+    for at, first in BACK_FROM.items():
+        start = jnp.where(group == at, first, start)
+    back = column >= start
+    ky = jnp.where(back, group + FRONT, group + 1) // 2
+    kx = jnp.where(back, GROUP - column, column + 1) // 2
     factor = jnp.where(ky * ky + kx * kx <= limit * limit, rate, 0.0)
     analysis = jnp.where(mine == 1, analysis, 0.0)
 
@@ -191,23 +223,18 @@
     lax.fori_loop(0, F, one, 0)
     tables[1].wait()
     high, low = split(jnp.concatenate([bands[tile] for tile in range(bands.shape[0])], axis=1))
-    both = dot(high, fx[...])
-    spectrum = both[:, :128] + both[:, 128:] + dot(low, fx[:, :128])
-    spectrum = pack([spectrum[F * slot : F * slot + F] for slot in range(SLOTS)])
+    both = dot(high, fx[...]) + dot(low, fx[...])
+    both = [both[:, 128 * way : 128 * way + 128] for way in range(2)]
+    both = [way + pltpu.roll(way, 128 - GROUP, 1) for way in both]
+    spectrum = pack([both[int(slot >= FRONT)][F * slot : F * slot + F] for slot in range(NK)])
     share[...] = factor * (analysis - spectrum)
     tables[2].wait()
     tables[3].wait()
 
 
 def nudge_kernel(levels, chunk, mine, other, field, iy, ix, out_hbm, out, bands, sem):
-    total = mine[...] + other[...]
-    group = lane_group((F, 128))
-    rows = []
-    for j in range(4):
-        for block in range(SLOTS // 4):
-            rows.append(jnp.where(group == j, total[:, 128 * block : 128 * block + 128], 0.0))
-    high, low = split(jnp.concatenate(rows, axis=0))
-    wide = dot(high, ix[:128]) + dot(high, ix[128:]) + dot(low, ix[:128])
+    high, low = split(unpack(mine[...] + other[...]))
+    wide = dot(high, ix[...]) + dot(low, ix[...])
     for tile in range(bands.shape[0]):
         bands[tile] = wide[:, 128 * tile : 128 * tile + 128]
     ny, nx = out.shape[1:]

time: 22.1 us -> 21.9 us (level)
  waiting for transfers between devices: 5.69 us -> 5.42 us
    ppermute x5, waiting for transfers between devices: 5.69 us -> 5.42 us  [swap(): lax.ppermute(value, ('gx', 'gy'), [(i, i ^ bits) for i in range(size)])]
where the time goes in v5:
time: 21.9 us; the launch traced here: 21.7 us
  Pallas kernels  8.2 us (37%)
  starting transfers between devices  8.09 us (37%)
  waiting for transfers between devices  5.42 us (25%)
    ppermute x5, starting transfers between devices, swap(): lax.ppermute(value, ('gx', 'gy'), [(i, i ^ bits) for i in range(size)])  8.09 us
    ppermute x5, waiting for transfers between devices, swap(): lax.ppermute(value, ('gx', 'gy'), [(i, i ^ bits) for i in range(size)])  5.42 us
    pallas_call x1, Pallas kernels, body(): pl.pallas_call(functools.partial(project_kernel, n_gy, levels), out_shape...  4.26 us
    pallas_call x1, Pallas kernels, body(): pl.pallas_call(functools.partial(nudge_kernel, levels, chunk), out_shape=...  3.94 us
  transfers between devices with their start and end apart: 5, of which 4 were waited for; matrix products, arithmetic and copies ran while one was open for 0% of the time, Pallas kernels for 0%

profile of v5, /device:TPU:0, one launch (start us, length us, event | category | flops | bytes accessed | tf_op | source)
XLA Modules:
  0.0 21.7 jit_solution(9052409592041802219)
XLA Ops:
  0.0 4.3 %project.1 = (f32[8,512]{1,0:T(8,128)S(1)}, f32[8,512,512]{2,1,0:T(8,128)S(1)}, bf16[512,128]{1,0:T(8,128)(2,1)S(1)}, bf16[256,512]{1,0:T(8,128)(2,1)S(1)}) custom-call(s32[1,2]{1,0:T(1,128)} %owner_hbm.1, s32[2,4]{1,0:T(2,128)} %cutoff_hbm.1, f32[2,4]{1,0:T(2,128)} %relax_hbm.1, f32[1,2,4,882]{3,2,1,0:T(4,128)} %era_hbm.1, f32[2,4,512,512]{3,2,1,0:T(8,128)} %field_hbm.1, ...), custom_call_target="tpu_custom_call" | custom-call | tf_op jit(solution)/shard_map/project/pallas_call | solution.py:289
  4.3 3.1 %collective-permute-start = (f32[8,512]{1,0:T(8,128)S(1)}, f32[8,512]{1,0:T(8,128)S(1)}, u32[]{:S(2)}, u32[]{:S(2)}) collective-permute-start(f32[8,512]{1,0:T(8,128)S(1)} %get-tuple-element.9), channel_id=1, source_target_pairs={{0,2},{2,0},{4,6},{6,4},{8,10},{10,8},{12,14},{14,12},{16,18},{18,... | collective-permute-start | bytes 49160 | tf_op jit(solution)/shard_map/ppermute | solution.py:280
  7.4 1.7 %collective-permute-done = f32[8,512]{1,0:T(8,128)S(1)} collective-permute-done((f32[8,512]{1,0:T(8,128)S(1)}, f32[8,512]{1,0:T(8,128)S(1)}, u32[]{:S(2)}, u32[]{:S(2)}) %collective-permute-start) | collective-permute-done | bytes 16416 | tf_op jit(solution)/shard_map/ppermute | solution.py:280
  9.1 0.3 %collective-permute-start.3 = (f32[8,512]{1,0:T(8,128)S(1)}, f32[8,512]{1,0:T(8,128)S(1)}, u32[]{:S(2)}, u32[]{:S(2)}) collective-permute-start(f32[8,512]{1,0:T(8,128)S(1)} %add.12), channel_id=1, source_target_pairs={{0,24},{2,26},{4,28},{6,30},{8,16},{10,18},{12,20},{14,22},{16,8},... | collective-permute-start | bytes 49160 | tf_op jit(solution)/shard_map/ppermute | solution.py:280
  9.3 1.8 %collective-permute-start.2 = (f32[8,512]{1,0:T(8,128)S(1)}, f32[8,512]{1,0:T(8,128)S(1)}, u32[]{:S(2)}, u32[]{:S(2)}) collective-permute-start(f32[8,512]{1,0:T(8,128)S(1)} %add.12), channel_id=1, source_target_pairs={{0,16},{2,18},{4,20},{6,22},{8,24},{10,26},{12,28},{14,30},{16,0},... | collective-permute-start | bytes 49160 | tf_op jit(solution)/shard_map/ppermute | solution.py:280
  11.1 0.0 collective-permute-start.1
  11.2 1.1 %collective-permute-done.3 = f32[8,512]{1,0:T(8,128)S(1)} collective-permute-done((f32[8,512]{1,0:T(8,128)S(1)}, f32[8,512]{1,0:T(8,128)S(1)}, u32[]{:S(2)}, u32[]{:S(2)}) %collective-permute-start.3) | collective-permute-done | bytes 16416 | tf_op jit(solution)/shard_map/ppermute | solution.py:280
  12.2 0.8 %collective-permute-done.2 = f32[8,512]{1,0:T(8,128)S(1)} collective-permute-done((f32[8,512]{1,0:T(8,128)S(1)}, f32[8,512]{1,0:T(8,128)S(1)}, u32[]{:S(2)}, u32[]{:S(2)}) %collective-permute-start.2) | collective-permute-done | bytes 16416 | tf_op jit(solution)/shard_map/ppermute | solution.py:280
  13.1 0.0 collective-permute-done.1
  13.1 2.9 %collective-permute-start.4 = (f32[8,512]{1,0:T(8,128)S(1)}, f32[8,512]{1,0:T(8,128)S(1)}, u32[]{:S(2)}, u32[]{:S(2)}) collective-permute-start(f32[8,512]{1,0:T(8,128)S(1)} %add_add_fusion.mine), channel_id=1, source_target_pairs={{0,4},{2,6},{4,0},{6,2},{8,12},{10,14},{12,8},{14,10},{16,20},{18,... | collective-permute-start | bytes 49160 | tf_op jit(solution)/shard_map/ppermute | solution.py:280
  16.0 1.8 %collective-permute-done.4.other = f32[8,512]{1,0:T(8,128)S(1)} collective-permute-done((f32[8,512]{1,0:T(8,128)S(1)}, f32[8,512]{1,0:T(8,128)S(1)}, u32[]{:S(2)}, u32[]{:S(2)}) %collective-permute-start.4) | collective-permute-done | bytes 16416 | tf_op jit(solution)/shard_map/ppermute | solution.py:280
  17.8 3.9 %nudge.1 = f32[2,4,512,512]{3,2,1,0:T(8,128)} custom-call(f32[8,512]{1,0:T(8,128)S(1)} %add_add_fusion.mine, f32[8,512]{1,0:T(8,128)S(1)} %collective-permute-done.4.other, f32[8,512,512]{2,1,0:T(8,128)S(1)} %get-tuple-element.10.field, bf16[512,128]{1,0:T(8,128)(2,1)S(1)} %get-tuple-element.11.iy, bf16[256,512]{1,0:T(8,128)(2,1)S(1)} %get-tuple-element.12.ix), custom_call_target="tpu_custom_call" | custom-call | tf_op jit(solution)/shard_map/nudge/pallas_call | solution.py:324
  (2 shorter events, 0.0 us)
Async XLA Ops:
  4.3 4.8 %collective-permute-start = (f32[8,512]{1,0:T(8,128)S(1)}, f32[8,512]{1,0:T(8,128)S(1)}, u32[]{:S(2)}, u32[]{:S(2)}) collective-permute-start(f32[8,512]{1,0:T(8,128)S(1)} %get-tuple-element.9), channel_id=1, source_target_pairs={{0,2},{2,0},{4,6},{6,4},{8,10},{10,8},{12,14},{14,12},{16,18},{18,... | collective-permute-start | bytes 49160 | tf_op jit(solution)/shard_map/ppermute | solution.py:280
  9.1 3.2 %collective-permute-start.3 = (f32[8,512]{1,0:T(8,128)S(1)}, f32[8,512]{1,0:T(8,128)S(1)}, u32[]{:S(2)}, u32[]{:S(2)}) collective-permute-start(f32[8,512]{1,0:T(8,128)S(1)} %add.12), channel_id=1, source_target_pairs={{0,24},{2,26},{4,28},{6,30},{8,16},{10,18},{12,20},{14,22},{16,8},... | collective-permute-start | bytes 49160 | tf_op jit(solution)/shard_map/ppermute | solution.py:280
  9.3 3.7 %collective-permute-start.2 = (f32[8,512]{1,0:T(8,128)S(1)}, f32[8,512]{1,0:T(8,128)S(1)}, u32[]{:S(2)}, u32[]{:S(2)}) collective-permute-start(f32[8,512]{1,0:T(8,128)S(1)} %add.12), channel_id=1, source_target_pairs={{0,16},{2,18},{4,20},{6,22},{8,24},{10,26},{12,28},{14,30},{16,0},... | collective-permute-start | bytes 49160 | tf_op jit(solution)/shard_map/ppermute | solution.py:280
  11.1 2.0 %collective-permute-start.1 = (f32[8,512]{1,0:T(8,128)S(1)}, f32[8,512]{1,0:T(8,128)S(1)}, u32[]{:S(2)}, u32[]{:S(2)}) collective-permute-start(f32[8,512]{1,0:T(8,128)S(1)} %add.12), channel_id=1, source_target_pairs={{0,8},{2,10},{4,12},{6,14},{8,0},{10,2},{12,4},{14,6},{16,24},{18,... | collective-permute-start | bytes 49160 | tf_op jit(solution)/shard_map/ppermute | solution.py:280
  13.1 4.7 %collective-permute-start.4 = (f32[8,512]{1,0:T(8,128)S(1)}, f32[8,512]{1,0:T(8,128)S(1)}, u32[]{:S(2)}, u32[]{:S(2)}) collective-permute-start(f32[8,512]{1,0:T(8,128)S(1)} %add_add_fusion.mine), channel_id=1, source_target_pairs={{0,4},{2,6},{4,0},{6,2},{8,12},{10,14},{12,8},{14,10},{16,20},{18,... | collective-permute-start | bytes 49160 | tf_op jit(solution)/shard_map/ppermute | solution.py:280

commit v6 on v5

--- a/solution.py
+++ b/solution.py
@@ -269,11 +269,11 @@
     return pltpu.with_memory_space_constraint(jnp.asarray(value), pltpu.HBM)
 
 
-def phases_of(n_gx, n_gy):
-    along_y = [[1 << bit] for bit in range(n_gy.bit_length() - 1)]
-    along_x = [[bits * n_gy for bits in range(1, min(n_gx, 4))]]
-    along_x += [[n_gy << bit] for bit in range(2, n_gx.bit_length() - 1)]
-    return along_y[:1] + along_x + along_y[1:]
+def partners_of(n_gx, n_gy):
+    core = n_gy
+    along_x = [core | n_gy << bit for bit in range(1, n_gx.bit_length() - 1)]
+    along_y = [core | 1 << bit for bit in range(n_gy.bit_length() - 1)]
+    return [core] + along_x + along_y
 
 
 def swap(value, size, bits):
@@ -313,12 +313,10 @@
         name="project",
     )(*(in_hbm(value) for value in (owner_map, cutoff, relax_rate, era_store, model_state, fy, fx, iy, ix)))
 
-    phases = phases_of(n_gx, n_gy)
-    for phase in phases[:-1]:
-        got = [swap(share, n_gx * n_gy, bits) for bits in phase]
-        for other in got:
-            share = share + other
-    other = sum(swap(share, n_gx * n_gy, bits) for bits in phases[-1])
+    steps = partners_of(n_gx, n_gy)
+    for bits in steps[:-1]:
+        share = share + swap(share, n_gx * n_gy, bits)
+    other = swap(share, n_gx * n_gy, steps[-1])
 
     chunk = min(ny, 256)
     nudged = pl.pallas_call(

time: 21.9 us -> 21.2 us (0.968)
  starting transfers between devices: 8.09 us -> 7.66 us
  waiting for transfers between devices: 5.42 us -> 5.17 us
    ppermute x5 -> x4, starting transfers between devices: 8.09 us -> 7.66 us  [swap(): lax.ppermute(value, ('gx', 'gy'), [(i, i ^ bits) for i in range(size)])]
    ppermute x5 -> x4, waiting for transfers between devices: 5.42 us -> 5.17 us  [swap(): lax.ppermute(value, ('gx', 'gy'), [(i, i ^ bits) for i in range(size)])]
  transfers between devices with their start and end apart: 5 -> 4, of which waited for: 4 -> 4; matrix products, arithmetic and copies ran while one was open for 0% -> 0% of each run, Pallas kernels for 0% -> 0%
where the time goes in v6:
time: 21.2 us; the launch traced here: 21.1 us
  Pallas kernels  8.2 us (39%)
  starting transfers between devices  7.66 us (36%)
  waiting for transfers between devices  5.17 us (24%)
    ppermute x4, starting transfers between devices, swap(): lax.ppermute(value, ('gx', 'gy'), [(i, i ^ bits) for i in range(size)])  7.66 us
    ppermute x4, waiting for transfers between devices, swap(): lax.ppermute(value, ('gx', 'gy'), [(i, i ^ bits) for i in range(size)])  5.17 us
    pallas_call x1, Pallas kernels, body(): pl.pallas_call(functools.partial(project_kernel, n_gy, levels), out_shape...  4.26 us
    pallas_call x1, Pallas kernels, body(): pl.pallas_call(functools.partial(nudge_kernel, levels, chunk), out_shape=...  3.94 us
  transfers between devices with their start and end apart: 4, of which 4 were waited for; matrix products, arithmetic and copies ran while one was open for 0% of the time, Pallas kernels for 0%

profile of v6, /device:TPU:0, one launch (start us, length us, event | category | flops | bytes accessed | tf_op | source)
XLA Modules:
  0.0 21.1 jit_solution(8444393965674147205)
XLA Ops:
  0.0 4.3 %project.1 = (f32[8,512]{1,0:T(8,128)S(1)}, f32[8,512,512]{2,1,0:T(8,128)S(1)}, bf16[512,128]{1,0:T(8,128)(2,1)S(1)}, bf16[256,512]{1,0:T(8,128)(2,1)S(1)}) custom-call(s32[1,2]{1,0:T(1,128)} %owner_hbm.1, s32[2,4]{1,0:T(2,128)} %cutoff_hbm.1, f32[2,4]{1,0:T(2,128)} %relax_hbm.1, f32[1,2,4,882]{3,2,1,0:T(4,128)} %era_hbm.1, f32[2,4,512,512]{3,2,1,0:T(8,128)} %field_hbm.1, ...), custom_call_target="tpu_custom_call" | custom-call | tf_op jit(solution)/shard_map/project/pallas_call | solution.py:289
  4.3 0.5 %collective-permute-start = (f32[8,512]{1,0:T(8,128)S(1)}, f32[8,512]{1,0:T(8,128)S(1)}, u32[]{:S(2)}, u32[]{:S(2)}) collective-permute-start(f32[8,512]{1,0:T(8,128)S(1)} %get-tuple-element.9), channel_id=1, source_target_pairs={{0,8},{2,10},{4,12},{6,14},{8,0},{10,2},{12,4},{14,6},{16,24},{18,... | collective-permute-start | bytes 49160 | tf_op jit(solution)/shard_map/ppermute | solution.py:280
  4.8 0.8 %collective-permute-done = f32[8,512]{1,0:T(8,128)S(1)} collective-permute-done((f32[8,512]{1,0:T(8,128)S(1)}, f32[8,512]{1,0:T(8,128)S(1)}, u32[]{:S(2)}, u32[]{:S(2)}) %collective-permute-start) | collective-permute-done | bytes 16416 | tf_op jit(solution)/shard_map/ppermute | solution.py:280
  5.6 2.6 %collective-permute-start.1 = (f32[8,512]{1,0:T(8,128)S(1)}, f32[8,512]{1,0:T(8,128)S(1)}, u32[]{:S(2)}, u32[]{:S(2)}) collective-permute-start(f32[8,512]{1,0:T(8,128)S(1)} %add.9), channel_id=1, source_target_pairs={{0,24},{2,26},{4,28},{6,30},{8,16},{10,18},{12,20},{14,22},{16,8},... | collective-permute-start | bytes 49160 | tf_op jit(solution)/shard_map/ppermute | solution.py:280
  8.3 1.4 %collective-permute-done.1 = f32[8,512]{1,0:T(8,128)S(1)} collective-permute-done((f32[8,512]{1,0:T(8,128)S(1)}, f32[8,512]{1,0:T(8,128)S(1)}, u32[]{:S(2)}, u32[]{:S(2)}) %collective-permute-start.1) | collective-permute-done | bytes 16416 | tf_op jit(solution)/shard_map/ppermute | solution.py:280
  9.7 1.8 %collective-permute-start.2 = (f32[8,512]{1,0:T(8,128)S(1)}, f32[8,512]{1,0:T(8,128)S(1)}, u32[]{:S(2)}, u32[]{:S(2)}) collective-permute-start(f32[8,512]{1,0:T(8,128)S(1)} %add.10), channel_id=1, source_target_pairs={{0,10},{2,8},{4,14},{6,12},{8,2},{10,0},{12,6},{14,4},{16,26},{18,... | collective-permute-start | bytes 49160 | tf_op jit(solution)/shard_map/ppermute | solution.py:280
  11.5 1.4 %collective-permute-done.2 = f32[8,512]{1,0:T(8,128)S(1)} collective-permute-done((f32[8,512]{1,0:T(8,128)S(1)}, f32[8,512]{1,0:T(8,128)S(1)}, u32[]{:S(2)}, u32[]{:S(2)}) %collective-permute-start.2) | collective-permute-done | bytes 16416 | tf_op jit(solution)/shard_map/ppermute | solution.py:280
  12.9 2.7 %collective-permute-start.3 = (f32[8,512]{1,0:T(8,128)S(1)}, f32[8,512]{1,0:T(8,128)S(1)}, u32[]{:S(2)}, u32[]{:S(2)}) collective-permute-start(f32[8,512]{1,0:T(8,128)S(1)} %add.11.mine), channel_id=1, source_target_pairs={{0,12},{2,14},{4,8},{6,10},{8,4},{10,6},{12,0},{14,2},{16,28},{18,... | collective-permute-start | bytes 49160 | tf_op jit(solution)/shard_map/ppermute | solution.py:280
  15.7 1.4 %collective-permute-done.3.other = f32[8,512]{1,0:T(8,128)S(1)} collective-permute-done((f32[8,512]{1,0:T(8,128)S(1)}, f32[8,512]{1,0:T(8,128)S(1)}, u32[]{:S(2)}, u32[]{:S(2)}) %collective-permute-start.3) | collective-permute-done | bytes 16416 | tf_op jit(solution)/shard_map/ppermute | solution.py:280
  17.1 3.9 %nudge.1 = f32[2,4,512,512]{3,2,1,0:T(8,128)} custom-call(f32[8,512]{1,0:T(8,128)S(1)} %add.11.mine, f32[8,512]{1,0:T(8,128)S(1)} %collective-permute-done.3.other, f32[8,512,512]{2,1,0:T(8,128)S(1)} %get-tuple-element.10.field, bf16[512,128]{1,0:T(8,128)(2,1)S(1)} %get-tuple-element.11.iy, bf16[256,512]{1,0:T(8,128)(2,1)S(1)} %get-tuple-element.12.ix), custom_call_target="tpu_custom_call" | custom-call | tf_op jit(solution)/shard_map/nudge/pallas_call | solution.py:322
  (3 shorter events, 0.0 us)
Async XLA Ops:
  4.3 1.4 %collective-permute-start = (f32[8,512]{1,0:T(8,128)S(1)}, f32[8,512]{1,0:T(8,128)S(1)}, u32[]{:S(2)}, u32[]{:S(2)}) collective-permute-start(f32[8,512]{1,0:T(8,128)S(1)} %get-tuple-element.9), channel_id=1, source_target_pairs={{0,8},{2,10},{4,12},{6,14},{8,0},{10,2},{12,4},{14,6},{16,24},{18,... | collective-permute-start | bytes 49160 | tf_op jit(solution)/shard_map/ppermute | solution.py:280
  5.6 4.1 %collective-permute-start.1 = (f32[8,512]{1,0:T(8,128)S(1)}, f32[8,512]{1,0:T(8,128)S(1)}, u32[]{:S(2)}, u32[]{:S(2)}) collective-permute-start(f32[8,512]{1,0:T(8,128)S(1)} %add.9), channel_id=1, source_target_pairs={{0,24},{2,26},{4,28},{6,30},{8,16},{10,18},{12,20},{14,22},{16,8},... | collective-permute-start | bytes 49160 | tf_op jit(solution)/shard_map/ppermute | solution.py:280
  9.7 3.2 %collective-permute-start.2 = (f32[8,512]{1,0:T(8,128)S(1)}, f32[8,512]{1,0:T(8,128)S(1)}, u32[]{:S(2)}, u32[]{:S(2)}) collective-permute-start(f32[8,512]{1,0:T(8,128)S(1)} %add.10), channel_id=1, source_target_pairs={{0,10},{2,8},{4,14},{6,12},{8,2},{10,0},{12,6},{14,4},{16,26},{18,... | collective-permute-start | bytes 49160 | tf_op jit(solution)/shard_map/ppermute | solution.py:280
  12.9 4.2 %collective-permute-start.3 = (f32[8,512]{1,0:T(8,128)S(1)}, f32[8,512]{1,0:T(8,128)S(1)}, u32[]{:S(2)}, u32[]{:S(2)}) collective-permute-start(f32[8,512]{1,0:T(8,128)S(1)} %add.11.mine), channel_id=1, source_target_pairs={{0,12},{2,14},{4,8},{6,10},{8,4},{10,6},{12,0},{14,2},{16,28},{18,... | collective-permute-start | bytes 49160 | tf_op jit(solution)/shard_map/ppermute | solution.py:280

commit v7 on v6

--- a/solution.py
+++ b/solution.py
@@ -233,16 +233,20 @@
 
 
 def nudge_kernel(levels, chunk, mine, other, field, iy, ix, out_hbm, out, bands, sem):
-    high, low = split(unpack(mine[...] + other[...]))
-    wide = dot(high, ix[...]) + dot(low, ix[...])
-    for tile in range(bands.shape[0]):
-        bands[tile] = wide[:, 128 * tile : 128 * tile + 128]
+    rows = unpack(mine[...] + other[...])
+    for tile in range(2):
+        bands[tile] = rows[:, 128 * tile : 128 * tile + 128]
     ny, nx = out.shape[1:]
     steps = ny // chunk
 
     def one(f, _):
-        band = [bands[tile, pl.ds(f, SLOTS, stride=F), :] for tile in range(bands.shape[0])]
-        band = jnp.concatenate(band, axis=1)
+        rows = [bands[tile, pl.ds(f, SLOTS, stride=F), :] for tile in range(2)]
+        rows = jnp.concatenate(rows, axis=1)
+        high = rows.astype(jnp.bfloat16).astype(jnp.float32)
+        pad = jnp.zeros((8, 256), jnp.float32)
+        rows = jnp.concatenate([high, pad, rows - high, pad], axis=0).astype(jnp.bfloat16)
+        wide = dot(rows, ix[...])
+        band = wide[:SLOTS] + wide[32 : 32 + SLOTS]
         high = band.astype(jnp.bfloat16).astype(jnp.float32)
         stacked = jnp.concatenate([high, high, band - high, jnp.zeros((128 - 3 * SLOTS, nx), jnp.float32)], axis=0)
         stacked = stacked.astype(jnp.bfloat16)
@@ -254,7 +258,7 @@
             ).start()
         return 0
 
-    lax.fori_loop(0, F, one, 0)
+    lax.fori_loop(0, F, one, 0, unroll=8)
 
     def end(n, _):
         f, step = n // steps, n % steps
@@ -326,7 +330,7 @@
         out_specs=hbm,
         scratch_shapes=[
             pltpu.VMEM((F, ny, nx), jnp.float32),
-            pltpu.VMEM((nx // 128, SLOTS * F, 128), jnp.float32),
+            pltpu.VMEM((2, SLOTS * F, 128), jnp.float32),
             pltpu.SemaphoreType.DMA((F * (ny // chunk),)),
         ],
         compiler_params=pltpu.CompilerParams(vmem_limit_bytes=30 * 2**20),

time: 21.2 us -> 21.1 us (level)
  no operation moved by 1% of the time
where the time goes in v7:
time: 21.1 us; the launch traced here: 20.9 us
  Pallas kernels  8.09 us (38%)
  starting transfers between devices  7.66 us (36%)
  waiting for transfers between devices  5.17 us (25%)
    ppermute x4, starting transfers between devices, swap(): lax.ppermute(value, ('gx', 'gy'), [(i, i ^ bits) for i in range(size)])  7.66 us
    ppermute x4, waiting for transfers between devices, swap(): lax.ppermute(value, ('gx', 'gy'), [(i, i ^ bits) for i in range(size)])  5.17 us
    pallas_call x1, Pallas kernels, body(): pl.pallas_call(functools.partial(project_kernel, n_gy, levels), out_shape...  4.26 us
    pallas_call x1, Pallas kernels, body(): pl.pallas_call(functools.partial(nudge_kernel, levels, chunk), out_shape=...  3.83 us
  transfers between devices with their start and end apart: 4, of which 4 were waited for; matrix products, arithmetic and copies ran while one was open for 0% of the time, Pallas kernels for 0%

profile of v7, /device:TPU:0, one launch (start us, length us, event | category | flops | bytes accessed | tf_op | source)
XLA Modules:
  0.0 20.9 jit_solution(16891681620252973737)
XLA Ops:
  0.0 4.3 %project.1 = (f32[8,512]{1,0:T(8,128)S(1)}, f32[8,512,512]{2,1,0:T(8,128)S(1)}, bf16[512,128]{1,0:T(8,128)(2,1)S(1)}, bf16[256,512]{1,0:T(8,128)(2,1)S(1)}) custom-call(s32[1,2]{1,0:T(1,128)} %owner_hbm.1, s32[2,4]{1,0:T(2,128)} %cutoff_hbm.1, f32[2,4]{1,0:T(2,128)} %relax_hbm.1, f32[1,2,4,882]{3,2,1,0:T(4,128)} %era_hbm.1, f32[2,4,512,512]{3,2,1,0:T(8,128)} %field_hbm.1, ...), custom_call_target="tpu_custom_call" | custom-call | tf_op jit(solution)/shard_map/project/pallas_call | solution.py:293
  4.3 0.5 %collective-permute-start = (f32[8,512]{1,0:T(8,128)S(1)}, f32[8,512]{1,0:T(8,128)S(1)}, u32[]{:S(2)}, u32[]{:S(2)}) collective-permute-start(f32[8,512]{1,0:T(8,128)S(1)} %get-tuple-element.9), channel_id=1, source_target_pairs={{0,8},{2,10},{4,12},{6,14},{8,0},{10,2},{12,4},{14,6},{16,24},{18,... | collective-permute-start | bytes 49160 | tf_op jit(solution)/shard_map/ppermute | solution.py:284
  4.8 0.8 %collective-permute-done = f32[8,512]{1,0:T(8,128)S(1)} collective-permute-done((f32[8,512]{1,0:T(8,128)S(1)}, f32[8,512]{1,0:T(8,128)S(1)}, u32[]{:S(2)}, u32[]{:S(2)}) %collective-permute-start) | collective-permute-done | bytes 16416 | tf_op jit(solution)/shard_map/ppermute | solution.py:284
  5.6 2.6 %collective-permute-start.1 = (f32[8,512]{1,0:T(8,128)S(1)}, f32[8,512]{1,0:T(8,128)S(1)}, u32[]{:S(2)}, u32[]{:S(2)}) collective-permute-start(f32[8,512]{1,0:T(8,128)S(1)} %add.9), channel_id=1, source_target_pairs={{0,24},{2,26},{4,28},{6,30},{8,16},{10,18},{12,20},{14,22},{16,8},... | collective-permute-start | bytes 49160 | tf_op jit(solution)/shard_map/ppermute | solution.py:284
  8.3 1.4 %collective-permute-done.1 = f32[8,512]{1,0:T(8,128)S(1)} collective-permute-done((f32[8,512]{1,0:T(8,128)S(1)}, f32[8,512]{1,0:T(8,128)S(1)}, u32[]{:S(2)}, u32[]{:S(2)}) %collective-permute-start.1) | collective-permute-done | bytes 16416 | tf_op jit(solution)/shard_map/ppermute | solution.py:284
  9.7 1.8 %collective-permute-start.2 = (f32[8,512]{1,0:T(8,128)S(1)}, f32[8,512]{1,0:T(8,128)S(1)}, u32[]{:S(2)}, u32[]{:S(2)}) collective-permute-start(f32[8,512]{1,0:T(8,128)S(1)} %add.10), channel_id=1, source_target_pairs={{0,10},{2,8},{4,14},{6,12},{8,2},{10,0},{12,6},{14,4},{16,26},{18,... | collective-permute-start | bytes 49160 | tf_op jit(solution)/shard_map/ppermute | solution.py:284
  11.5 1.4 %collective-permute-done.2 = f32[8,512]{1,0:T(8,128)S(1)} collective-permute-done((f32[8,512]{1,0:T(8,128)S(1)}, f32[8,512]{1,0:T(8,128)S(1)}, u32[]{:S(2)}, u32[]{:S(2)}) %collective-permute-start.2) | collective-permute-done | bytes 16416 | tf_op jit(solution)/shard_map/ppermute | solution.py:284
  12.9 2.7 %collective-permute-start.3 = (f32[8,512]{1,0:T(8,128)S(1)}, f32[8,512]{1,0:T(8,128)S(1)}, u32[]{:S(2)}, u32[]{:S(2)}) collective-permute-start(f32[8,512]{1,0:T(8,128)S(1)} %add.11.mine), channel_id=1, source_target_pairs={{0,12},{2,14},{4,8},{6,10},{8,4},{10,6},{12,0},{14,2},{16,28},{18,... | collective-permute-start | bytes 49160 | tf_op jit(solution)/shard_map/ppermute | solution.py:284
  15.7 1.4 %collective-permute-done.3.other = f32[8,512]{1,0:T(8,128)S(1)} collective-permute-done((f32[8,512]{1,0:T(8,128)S(1)}, f32[8,512]{1,0:T(8,128)S(1)}, u32[]{:S(2)}, u32[]{:S(2)}) %collective-permute-start.3) | collective-permute-done | bytes 16416 | tf_op jit(solution)/shard_map/ppermute | solution.py:284
  17.1 3.8 %nudge.1 = f32[2,4,512,512]{3,2,1,0:T(8,128)} custom-call(f32[8,512]{1,0:T(8,128)S(1)} %add.11.mine, f32[8,512]{1,0:T(8,128)S(1)} %collective-permute-done.3.other, f32[8,512,512]{2,1,0:T(8,128)S(1)} %get-tuple-element.10.field, bf16[512,128]{1,0:T(8,128)(2,1)S(1)} %get-tuple-element.11.iy, bf16[256,512]{1,0:T(8,128)(2,1)S(1)} %get-tuple-element.12.ix), custom_call_target="tpu_custom_call" | custom-call | tf_op jit(solution)/shard_map/nudge/pallas_call | solution.py:326
  (3 shorter events, 0.0 us)
Async XLA Ops:
  4.3 1.4 %collective-permute-start = (f32[8,512]{1,0:T(8,128)S(1)}, f32[8,512]{1,0:T(8,128)S(1)}, u32[]{:S(2)}, u32[]{:S(2)}) collective-permute-start(f32[8,512]{1,0:T(8,128)S(1)} %get-tuple-element.9), channel_id=1, source_target_pairs={{0,8},{2,10},{4,12},{6,14},{8,0},{10,2},{12,4},{14,6},{16,24},{18,... | collective-permute-start | bytes 49160 | tf_op jit(solution)/shard_map/ppermute | solution.py:284
  5.6 4.1 %collective-permute-start.1 = (f32[8,512]{1,0:T(8,128)S(1)}, f32[8,512]{1,0:T(8,128)S(1)}, u32[]{:S(2)}, u32[]{:S(2)}) collective-permute-start(f32[8,512]{1,0:T(8,128)S(1)} %add.9), channel_id=1, source_target_pairs={{0,24},{2,26},{4,28},{6,30},{8,16},{10,18},{12,20},{14,22},{16,8},... | collective-permute-start | bytes 49160 | tf_op jit(solution)/shard_map/ppermute | solution.py:284
  9.7 3.2 %collective-permute-start.2 = (f32[8,512]{1,0:T(8,128)S(1)}, f32[8,512]{1,0:T(8,128)S(1)}, u32[]{:S(2)}, u32[]{:S(2)}) collective-permute-start(f32[8,512]{1,0:T(8,128)S(1)} %add.10), channel_id=1, source_target_pairs={{0,10},{2,8},{4,14},{6,12},{8,2},{10,0},{12,6},{14,4},{16,26},{18,... | collective-permute-start | bytes 49160 | tf_op jit(solution)/shard_map/ppermute | solution.py:284
  12.9 4.2 %collective-permute-start.3 = (f32[8,512]{1,0:T(8,128)S(1)}, f32[8,512]{1,0:T(8,128)S(1)}, u32[]{:S(2)}, u32[]{:S(2)}) collective-permute-start(f32[8,512]{1,0:T(8,128)S(1)} %add.11.mine), channel_id=1, source_target_pairs={{0,12},{2,14},{4,8},{6,10},{8,4},{10,6},{12,0},{14,2},{16,28},{18,... | collective-permute-start | bytes 49160 | tf_op jit(solution)/shard_map/ppermute | solution.py:284

commit v8 on v7

--- a/solution.py
+++ b/solution.py
@@ -220,7 +220,7 @@
             bands[tile, pl.ds(f, SLOTS, stride=F), :] = band[:, 128 * tile : 128 * tile + 128]
         return 0
 
-    lax.fori_loop(0, F, one, 0)
+    lax.fori_loop(0, F, one, 0, unroll=2)
     tables[1].wait()
     high, low = split(jnp.concatenate([bands[tile] for tile in range(bands.shape[0])], axis=1))
     both = dot(high, fx[...]) + dot(low, fx[...])

time: 21.1 us -> 21.1 us (level)
  no operation moved by 1% of the time
where the time goes in v8:
time: 21.1 us; the launch traced here: 20.9 us
  Pallas kernels  8.09 us (38%)
  starting transfers between devices  7.66 us (36%)
  waiting for transfers between devices  5.17 us (25%)
    ppermute x4, starting transfers between devices, swap(): lax.ppermute(value, ('gx', 'gy'), [(i, i ^ bits) for i in range(size)])  7.66 us
    ppermute x4, waiting for transfers between devices, swap(): lax.ppermute(value, ('gx', 'gy'), [(i, i ^ bits) for i in range(size)])  5.17 us
    pallas_call x1, Pallas kernels, body(): pl.pallas_call(functools.partial(project_kernel, n_gy, levels), out_shape...  4.26 us
    pallas_call x1, Pallas kernels, body(): pl.pallas_call(functools.partial(nudge_kernel, levels, chunk), out_shape=...  3.83 us
  transfers between devices with their start and end apart: 4, of which 4 were waited for; matrix products, arithmetic and copies ran while one was open for 0% of the time, Pallas kernels for 0%

profile of v8, /device:TPU:0, one launch (start us, length us, event | category | flops | bytes accessed | tf_op | source)
XLA Modules:
  0.0 20.9 jit_solution(4903554848690396745)
XLA Ops:
  0.0 4.3 %project.1 = (f32[8,512]{1,0:T(8,128)S(1)}, f32[8,512,512]{2,1,0:T(8,128)S(1)}, bf16[512,128]{1,0:T(8,128)(2,1)S(1)}, bf16[256,512]{1,0:T(8,128)(2,1)S(1)}) custom-call(s32[1,2]{1,0:T(1,128)} %owner_hbm.1, s32[2,4]{1,0:T(2,128)} %cutoff_hbm.1, f32[2,4]{1,0:T(2,128)} %relax_hbm.1, f32[1,2,4,882]{3,2,1,0:T(4,128)} %era_hbm.1, f32[2,4,512,512]{3,2,1,0:T(8,128)} %field_hbm.1, ...), custom_call_target="tpu_custom_call" | custom-call | tf_op jit(solution)/shard_map/project/pallas_call | solution.py:293
  4.3 0.5 %collective-permute-start = (f32[8,512]{1,0:T(8,128)S(1)}, f32[8,512]{1,0:T(8,128)S(1)}, u32[]{:S(2)}, u32[]{:S(2)}) collective-permute-start(f32[8,512]{1,0:T(8,128)S(1)} %get-tuple-element.9), channel_id=1, source_target_pairs={{0,8},{2,10},{4,12},{6,14},{8,0},{10,2},{12,4},{14,6},{16,24},{18,... | collective-permute-start | bytes 49160 | tf_op jit(solution)/shard_map/ppermute | solution.py:284
  4.8 0.8 %collective-permute-done = f32[8,512]{1,0:T(8,128)S(1)} collective-permute-done((f32[8,512]{1,0:T(8,128)S(1)}, f32[8,512]{1,0:T(8,128)S(1)}, u32[]{:S(2)}, u32[]{:S(2)}) %collective-permute-start) | collective-permute-done | bytes 16416 | tf_op jit(solution)/shard_map/ppermute | solution.py:284
  5.6 2.6 %collective-permute-start.1 = (f32[8,512]{1,0:T(8,128)S(1)}, f32[8,512]{1,0:T(8,128)S(1)}, u32[]{:S(2)}, u32[]{:S(2)}) collective-permute-start(f32[8,512]{1,0:T(8,128)S(1)} %add.9), channel_id=1, source_target_pairs={{0,24},{2,26},{4,28},{6,30},{8,16},{10,18},{12,20},{14,22},{16,8},... | collective-permute-start | bytes 49160 | tf_op jit(solution)/shard_map/ppermute | solution.py:284
  8.3 1.4 %collective-permute-done.1 = f32[8,512]{1,0:T(8,128)S(1)} collective-permute-done((f32[8,512]{1,0:T(8,128)S(1)}, f32[8,512]{1,0:T(8,128)S(1)}, u32[]{:S(2)}, u32[]{:S(2)}) %collective-permute-start.1) | collective-permute-done | bytes 16416 | tf_op jit(solution)/shard_map/ppermute | solution.py:284
  9.7 1.8 %collective-permute-start.2 = (f32[8,512]{1,0:T(8,128)S(1)}, f32[8,512]{1,0:T(8,128)S(1)}, u32[]{:S(2)}, u32[]{:S(2)}) collective-permute-start(f32[8,512]{1,0:T(8,128)S(1)} %add.10), channel_id=1, source_target_pairs={{0,10},{2,8},{4,14},{6,12},{8,2},{10,0},{12,6},{14,4},{16,26},{18,... | collective-permute-start | bytes 49160 | tf_op jit(solution)/shard_map/ppermute | solution.py:284
  11.5 1.4 %collective-permute-done.2 = f32[8,512]{1,0:T(8,128)S(1)} collective-permute-done((f32[8,512]{1,0:T(8,128)S(1)}, f32[8,512]{1,0:T(8,128)S(1)}, u32[]{:S(2)}, u32[]{:S(2)}) %collective-permute-start.2) | collective-permute-done | bytes 16416 | tf_op jit(solution)/shard_map/ppermute | solution.py:284
  12.9 2.7 %collective-permute-start.3 = (f32[8,512]{1,0:T(8,128)S(1)}, f32[8,512]{1,0:T(8,128)S(1)}, u32[]{:S(2)}, u32[]{:S(2)}) collective-permute-start(f32[8,512]{1,0:T(8,128)S(1)} %add.11.mine), channel_id=1, source_target_pairs={{0,12},{2,14},{4,8},{6,10},{8,4},{10,6},{12,0},{14,2},{16,28},{18,... | collective-permute-start | bytes 49160 | tf_op jit(solution)/shard_map/ppermute | solution.py:284
  15.7 1.4 %collective-permute-done.3.other = f32[8,512]{1,0:T(8,128)S(1)} collective-permute-done((f32[8,512]{1,0:T(8,128)S(1)}, f32[8,512]{1,0:T(8,128)S(1)}, u32[]{:S(2)}, u32[]{:S(2)}) %collective-permute-start.3) | collective-permute-done | bytes 16416 | tf_op jit(solution)/shard_map/ppermute | solution.py:284
  17.1 3.8 %nudge.1 = f32[2,4,512,512]{3,2,1,0:T(8,128)} custom-call(f32[8,512]{1,0:T(8,128)S(1)} %add.11.mine, f32[8,512]{1,0:T(8,128)S(1)} %collective-permute-done.3.other, f32[8,512,512]{2,1,0:T(8,128)S(1)} %get-tuple-element.10.field, bf16[512,128]{1,0:T(8,128)(2,1)S(1)} %get-tuple-element.11.iy, bf16[256,512]{1,0:T(8,128)(2,1)S(1)} %get-tuple-element.12.ix), custom_call_target="tpu_custom_call" | custom-call | tf_op jit(solution)/shard_map/nudge/pallas_call | solution.py:326
  (3 shorter events, 0.0 us)
Async XLA Ops:
  4.3 1.4 %collective-permute-start = (f32[8,512]{1,0:T(8,128)S(1)}, f32[8,512]{1,0:T(8,128)S(1)}, u32[]{:S(2)}, u32[]{:S(2)}) collective-permute-start(f32[8,512]{1,0:T(8,128)S(1)} %get-tuple-element.9), channel_id=1, source_target_pairs={{0,8},{2,10},{4,12},{6,14},{8,0},{10,2},{12,4},{14,6},{16,24},{18,... | collective-permute-start | bytes 49160 | tf_op jit(solution)/shard_map/ppermute | solution.py:284
  5.6 4.1 %collective-permute-start.1 = (f32[8,512]{1,0:T(8,128)S(1)}, f32[8,512]{1,0:T(8,128)S(1)}, u32[]{:S(2)}, u32[]{:S(2)}) collective-permute-start(f32[8,512]{1,0:T(8,128)S(1)} %add.9), channel_id=1, source_target_pairs={{0,24},{2,26},{4,28},{6,30},{8,16},{10,18},{12,20},{14,22},{16,8},... | collective-permute-start | bytes 49160 | tf_op jit(solution)/shard_map/ppermute | solution.py:284
  9.7 3.2 %collective-permute-start.2 = (f32[8,512]{1,0:T(8,128)S(1)}, f32[8,512]{1,0:T(8,128)S(1)}, u32[]{:S(2)}, u32[]{:S(2)}) collective-permute-start(f32[8,512]{1,0:T(8,128)S(1)} %add.10), channel_id=1, source_target_pairs={{0,10},{2,8},{4,14},{6,12},{8,2},{10,0},{12,6},{14,4},{16,26},{18,... | collective-permute-start | bytes 49160 | tf_op jit(solution)/shard_map/ppermute | solution.py:284
  12.9 4.2 %collective-permute-start.3 = (f32[8,512]{1,0:T(8,128)S(1)}, f32[8,512]{1,0:T(8,128)S(1)}, u32[]{:S(2)}, u32[]{:S(2)}) collective-permute-start(f32[8,512]{1,0:T(8,128)S(1)} %add.11.mine), channel_id=1, source_target_pairs={{0,12},{2,14},{4,8},{6,10},{8,4},{10,6},{12,0},{14,2},{16,28},{18,... | collective-permute-start | bytes 49160 | tf_op jit(solution)/shard_map/ppermute | solution.py:284
